TPU v7x, 128 devices: a whole 4x4x4 slice. The times are simulated.
128 devices in a mesh: node: 16 (over z, y), local: 8 (over x, core).
Axes of the slice: x: 4, y: 4, z: 4, core: 2. Of those that a mesh axis runs over, the one named last changes fastest.
Arguments:
- tokens: bfloat16 [8192, 3584], P(('node', 'local')), may hold values from -6 to 6
- expert_ids: int32 [8192, 8], P(('node', 'local')), may hold values from 0 to 127, as said below
- gate_weights: bfloat16 [8192, 8], P(('node', 'local')), may hold values from 0.099609375 to 1
- expert_gate: bfloat16 [128, 3584, 1024], P(('node', 'local')), may hold values from -0.09375 to 0.09375
- expert_up: bfloat16 [128, 3584, 1024], P(('node', 'local')), may hold values from -0.09375 to 0.09375
- expert_down: bfloat16 [128, 1024, 3584], P(('node', 'local')), may hold values from -0.1875 to 0.1875
- shared_gate: bfloat16 [3584, 1024], P(None, 'local'), may hold values from -0.09375 to 0.09375
- shared_up: bfloat16 [3584, 1024], P(None, 'local'), may hold values from -0.09375 to 0.09375
- shared_down: bfloat16 [1024, 3584], P('local'), may hold values from -0.1875 to 0.1875
Outputs:
- mixed: bfloat16 [8192, 3584], P(('node', 'local'))
Inputs may be any that keep to these rules, and one draw needn't show every extreme that they name: `expert_ids`: expert e lives on node e // 8. Entries 2j and 2j + 1 of a row name two different experts of one node, and the 4 nodes of a row differ. Among the 64 rows of one device, half of the nodes receive exactly 24 rows and the other half exactly 8; the rows of one device that reach one node name each expert of that node equally often, so at most 6 rows of one device name one expert, and exactly that many for the busier nodes.
All inputs are finite; a program needn't handle non-finite values.
Results may differ from a plain program's by a relative error of at most 0.013.
Values may be sent and summed in bfloat16 or wider, within the bound.
A program may use at most 128 MiB of HBM per device.

v0:
```python
import jax
import jax.numpy as jnp
from jax import lax
from jax.sharding import PartitionSpec as P

TOP = 8
NODES_TOK = 4


def expert_sum(inputs, gate_matrix, up_matrix, down_matrix):
    gate_part = jnp.dot(inputs, gate_matrix, preferred_element_type=jnp.float32)
    up_part = jnp.dot(inputs, up_matrix, preferred_element_type=jnp.float32)
    hidden = (jax.nn.silu(gate_part) * up_part).astype(jnp.bfloat16)
    return jnp.dot(hidden, down_matrix, preferred_element_type=jnp.float32)


def exclusive_rank(labels, label_count):
    matches = (labels[:, None] == jnp.arange(label_count, dtype=jnp.int32)[None, :]).astype(
        jnp.int32
    )
    earlier = jnp.cumsum(matches, axis=0) - matches
    return jnp.sum(earlier * matches, axis=1)


def on_device(
    tokens,
    expert_ids,
    gate_weights,
    expert_gate,
    expert_up,
    expert_down,
    shared_gate,
    shared_up,
    shared_down,
):
    node_count = lax.axis_size("node")
    local_count = lax.axis_size("local")
    device_count = node_count * local_count
    token_count = tokens.shape[0]
    model_width = tokens.shape[1]
    mean_load = 4 * token_count // node_count
    node_cap = 3 * mean_load // 2
    expert_cap = 2 * node_cap // local_count
    gate_matrix = expert_gate[0]
    up_matrix = expert_up[0]
    down_matrix = expert_down[0]
    shared_terms = expert_sum(
        lax.all_gather(tokens, "local", axis=0, tiled=True), shared_gate, shared_up, shared_down
    )
    shared_out = lax.psum_scatter(
        shared_terms.astype(jnp.bfloat16), "local", scatter_dimension=0, tiled=True
    ).astype(jnp.float32)
    flat_ids = expert_ids.reshape(-1)
    slot_total = device_count * expert_cap
    slot_index = flat_ids * expert_cap + exclusive_rank(flat_ids, device_count)
    placed = slot_index[:, None] == jnp.arange(slot_total, dtype=jnp.int32)[None, :]
    pick_rows = jnp.any(placed.reshape(token_count, TOP, slot_total), axis=1).T.astype(jnp.bfloat16)
    outgoing = jnp.dot(pick_rows, tokens, preferred_element_type=jnp.float32).astype(jnp.bfloat16)
    received = lax.all_to_all(
        outgoing.reshape(device_count, expert_cap, model_width),
        ("node", "local"),
        split_axis=0,
        concat_axis=0,
        tiled=True,
    )
    results = expert_sum(received.reshape(-1, model_width), gate_matrix, up_matrix, down_matrix)
    results = results.astype(jnp.bfloat16).reshape(received.shape)
    returned = lax.all_to_all(results, ("node", "local"), split_axis=0, concat_axis=0, tiled=True)
    gate_flat = gate_weights.reshape(-1, 1).astype(jnp.float32)
    weighted = (
        jnp.where(placed, gate_flat, 0.0)
        .reshape(token_count, NODES_TOK, 2, slot_total)
        .sum(axis=2)
        .astype(jnp.bfloat16)
    )
    node_partial = jnp.einsum(
        "tjs,sd->jtd",
        weighted,
        returned.reshape(slot_total, model_width),
        preferred_element_type=jnp.float32,
    ).astype(jnp.bfloat16)
    routed = jnp.sum(node_partial.astype(jnp.float32), axis=0)
    return (shared_out + routed).astype(jnp.bfloat16)


def solution(mesh):
    in_specs = (
        P(("node", "local"), None),
        P(("node", "local"), None),
        P(("node", "local"), None),
        P(("node", "local"), None, None),
        P(("node", "local"), None, None),
        P(("node", "local"), None, None),
        P(None, "local"),
        P(None, "local"),
        P("local", None),
    )
    out_specs = P(("node", "local"), None)
    return jax.shard_map(
        on_device, mesh=mesh, in_specs=in_specs, out_specs=out_specs, check_vma=False
    )
```

profile of v0, /device:TPU:9, one launch (start us, length us, event | category | flops | bytes accessed | tf_op | source)
XLA Modules:
  0.0 310.6 jit_solution(17447875298531054208)
XLA Ops:
  6.5 0.9 copy.35
  7.7 0.2 fusion.22
  8.0 0.2 fusion.21
  8.4 0.7 broadcast_multiply_fusion
  9.2 0.5 fusion.16
  9.7 5.0 %convolution_convert_fusion = bf16[768,3584]{1,0:T(8,128)(2,1)} fusion(pred[64,768]{1,0:T(8,128)(4,1)S(1)} %fusion.16, bf16[64,3584]{1,0:T(8,128)(2,1)} %param.9), kind=kOutput, calls=%fused_computation.6 | convolution fusion | flops 355074048 | bytes 6012928 | tf_op jit(solution)/shard_map/dot_general | solution.py:58
  14.8 9.6 %reshape.76 = bf16[128,6,3584]{2,1,0:T(8,128)(2,1)} reshape(bf16[768,3584]{1,0:T(8,128)(2,1)} %convolution_convert_fusion) | data formatting | bytes 11010048 | tf_op jit(solution)/shard_map/reshape | solution.py:60
  24.3 11.2 %all-to-all-start = ((bf16[128,6,3584]{2,1,0:T(8,128)(2,1)}), bf16[128,6,3584]{2,1,0:T(8,128)(2,1)}, u32[]{:S(2)}, u32[]{:S(2)}) async-start(bf16[128,6,3584]{2,1,0:T(8,128)(2,1)} %reshape.76), calls=%async_computation.1 | async-start | bytes 14680064 | tf_op jit(solution)/shard_map/all_to_all | solution.py:59
  35.6 0.7 all-gather.2.cloned.1.call-update
  36.3 0.2 reduce-scatter.2.cloned.1.call-start
  36.5 98.1 %all-to-all-done = bf16[128,6,3584]{2,1,0:T(8,128)(2,1)} async-done(((bf16[128,6,3584]{2,1,0:T(8,128)(2,1)}), bf16[128,6,3584]{2,1,0:T(8,128)(2,1)}, u32[]{:S(2)}, u32[]{:S(2)}) %all-to-all-start) | async-done | bytes 5505056 | tf_op jit(solution)/shard_map/all_to_all | solution.py:59
  134.6 9.7 %reshape.77 = bf16[768,3584]{1,0:T(8,128)(2,1)} reshape(bf16[128,6,3584]{2,1,0:T(8,128)(2,1)} %all-to-all-done) | data formatting | bytes 11010048 | tf_op jit(solution)/shard_map/reshape | solution.py:66
  144.2 11.0 %fusion.2 = f32[768,1024]{1,0:T(8,128)} fusion(bf16[768,3584]{1,0:T(8,128)(2,1)} %reshape.77, bf16[1,3584,1024]{2,1,0:T(8,128)(2,1)} %param.13), kind=kOutput, calls=%fused_computation.2 | convolution fusion | flops 5637144576 | bytes 15990784 | tf_op jit(solution)/shard_map/dot_general | solution.py:12
  155.2 3.1 %fusion.34 = f32[512,128]{1,0:T(8,128)S(1)} fusion(bf16[512,3584]{1,0:T(8,128)(2,1)} %all-gather.2.cloned.1.call-done, bf16[3584,128]{1,0:T(8,128)(2,1)S(1)} %copy-done.3), kind=kOutput, calls=%fused_computation.43 | convolution fusion | flops 469762048 | bytes 4849664 | tf_op jit(solution)/shard_map/dot_general | solution.py:11
  158.4 7.8 %convolution_convert_fusion.1 = bf16[512,3584]{1,0:T(8,128)(2,1)} fusion(bf16[128,3584]{1,0:T(8,128)(2,1)S(1)} %copy-done, bf16[512,3584]{1,0:T(8,128)(2,1)} %all-gather.2.cloned.1.call-done, bf16[3584,128]{1,0:T(8,128)(2,1)S(1)} %copy-done.2, f32[512,128]{1,0:T(8,128)S(1)} %fusion.34), kind=kOutput, calls=%fused_computation.8 | convolution fusion | flops 941752320 | bytes 9437184 | tf_op jit(solution)/shard_map/dot_general | solution.py:14
  166.2 20.0 %fusion.6 = bf16[768,3584]{1,0:T(8,128)(2,1)} fusion(bf16[1,1024,3584]{2,1,0:T(8,128)(2,1)} %param.14, f32[768,1024]{1,0:T(8,128)} %fusion.2, bf16[768,3584]{1,0:T(8,128)(2,1)} %reshape.77, bf16[1,3584,1024]{2,1,0:T(8,128)(2,1)} %param.12), kind=kOutput, calls=%fused_computation.7 | convolution fusion | flops 11281760256 | bytes 28835840 | tf_op jit(solution)/shard_map/dot_general | solution.py:14
  186.2 9.6 %reshape.78 = bf16[128,6,3584]{2,1,0:T(8,128)(2,1)} reshape(bf16[768,3584]{1,0:T(8,128)(2,1)} %fusion.6) | data formatting | bytes 11010048 | tf_op jit(solution)/shard_map/reshape | solution.py:67
  195.9 8.1 %all-to-all-start.1 = ((bf16[128,6,3584]{2,1,0:T(8,128)(2,1)}), bf16[128,6,3584]{2,1,0:T(8,128)(2,1)}, u32[]{:S(2)}, u32[]{:S(2)}) async-start(bf16[128,6,3584]{2,1,0:T(8,128)(2,1)} %reshape.78), calls=%async_computation.2 | async-start | bytes 14680064 | tf_op jit(solution)/shard_map/all_to_all | solution.py:68
  204.0 0.2 reduce_sum.35
  204.3 0.2 select_reduce_fusion
  204.5 83.3 %all-to-all-done.1 = bf16[128,6,3584]{2,1,0:T(8,128)(2,1)} async-done(((bf16[128,6,3584]{2,1,0:T(8,128)(2,1)}), bf16[128,6,3584]{2,1,0:T(8,128)(2,1)}, u32[]{:S(2)}, u32[]{:S(2)}) %all-to-all-start.1) | async-done | bytes 5505056 | tf_op jit(solution)/shard_map/all_to_all | solution.py:68
  287.9 9.7 %reshape.81 = bf16[768,3584,1]{1,0,2:T(8,128)(2,1)} reshape(bf16[128,6,3584]{2,1,0:T(8,128)(2,1)} %all-to-all-done.1) | data formatting | bytes 11010048 | tf_op jit(solution)/shard_map/reshape | solution.py:79
  297.5 4.3 %fusion.14 = f32[3584,64]{0,1:T(8,128)S(1)} fusion(bf16[768,3584,1]{1,0,2:T(8,128)(2,1)} %reshape.81, bf16[64,4,768]{2,0,1:T(8,128)(2,1)S(1)} %select_reduce_fusion), kind=kOutput, calls=%fused_computation.12 | convolution fusion | flops 1411809280 | bytes 6815744 | tf_op jit(solution)/shard_map/tjs,sd->jtd/dot_general | solution.py:76
  301.9 1.9 fusion.18
  (29 shorter events, 0.8 us)
Async XLA Ops:
  6.5 151.9 %copy-start = (bf16[128,3584]{1,0:T(8,128)(2,1)S(1)}, bf16[128,3584]{1,0:T(8,128)(2,1)}, u32[]{:S(2)}) copy-start(bf16[128,3584]{1,0:T(8,128)(2,1)} %param.17) | copy-start | bytes 2752516
  24.3 110.2 %all-to-all-start = ((bf16[128,6,3584]{2,1,0:T(8,128)(2,1)}), bf16[128,6,3584]{2,1,0:T(8,128)(2,1)}, u32[]{:S(2)}, u32[]{:S(2)}) async-start(bf16[128,6,3584]{2,1,0:T(8,128)(2,1)} %reshape.76), calls=%async_computation.1 | async-start | bytes 14680064 | tf_op jit(solution)/shard_map/all_to_all | solution.py:59
  35.5 119.7 %all-gather.2.cloned.1.call-start = ((), (), s32[]{:S(2)}) async-start(), calls=%async_computation.3 | async-start | bytes 4128768 | tf_op jit(solution)/shard_map/all_gather | solution.py:48
  36.3 265.6 %reduce-scatter.2.cloned.1.call-start = ((), (), s32[]{:S(2)}) async-start(), calls=%async_computation.4 | async-start | bytes 4128768 | tf_op jit(solution)/shard_map/reduce_scatter | solution.py:50
  144.2 11.0 %copy-start.3 = (bf16[3584,128]{1,0:T(8,128)(2,1)S(1)}, bf16[3584,128]{1,0:T(8,128)(2,1)}, u32[]{:S(2)}) copy-start(bf16[3584,128]{1,0:T(8,128)(2,1)} %param.15) | copy-start | bytes 2752516
  144.2 14.2 %copy-start.2 = (bf16[3584,128]{1,0:T(8,128)(2,1)S(1)}, bf16[3584,128]{1,0:T(8,128)(2,1)}, u32[]{:S(2)}) copy-start(bf16[3584,128]{1,0:T(8,128)(2,1)} %param.16) | copy-start | bytes 2752516
  195.9 8.4 %copy-start.4 = (bf16[64,8]{0,1:T(8,128)(2,1)S(1)}, bf16[64,8]{0,1:T(8,128)(2,1)}, u32[]{:S(2)}) copy-start(bf16[64,8]{0,1:T(8,128)(2,1)} %param.11) | copy-start | bytes 3076
  195.9 92.0 %all-to-all-start.1 = ((bf16[128,6,3584]{2,1,0:T(8,128)(2,1)}), bf16[128,6,3584]{2,1,0:T(8,128)(2,1)}, u32[]{:S(2)}, u32[]{:S(2)}) async-start(bf16[128,6,3584]{2,1,0:T(8,128)(2,1)} %reshape.78), calls=%async_computation.2 | async-start | bytes 14680064 | tf_op jit(solution)/shard_map/all_to_all | solution.py:68
  297.5 6.2 %copy-start.1 = (bf16[128,3584]{1,0:T(8,128)(2,1)S(1)}, bf16[128,3584]{1,0:T(8,128)(2,1)}, u32[]{:S(2)}) copy-start(bf16[128,3584]{1,0:T(8,128)(2,1)} %param.17) | copy-start | bytes 2752516
Sparse Core Ops, SparseCore 0:
  38.0 61.3 all-gather.1
  166.3 31.6 reduce-scatter.1
where the time goes:
time: 316 us; the launch traced here: 311 us
  waiting for transfers between devices  182 us (58%)
  matrix products  51.3 us (16%)
  local copies, waits for them, and re-layouts  40.2 us (13%)
  starting transfers between devices  19.5 us (6%)
  between operations  13.5 us (4%)
  other arithmetic  3.85 us (1%)
    all_to_all x1, waiting for transfers between devices, on_device(): lax.all_to_all(outgoing.reshape(device_count, expert_cap, model_width), (...  98.1 us
    all_to_all x1, waiting for transfers between devices, on_device(): lax.all_to_all(results, ('node', 'local'), split_axis=0, concat_axis=0, t...  83.3 us
    dot_general x2, matrix products, expert_sum(): return jnp.dot(hidden, down_matrix, preferred_element_type=jnp.float32)  27.8 us
    all_to_all x1, starting transfers between devices, on_device(): lax.all_to_all(outgoing.reshape(device_count, expert_cap, model_width), (...  11.2 us
    dot_general x1, matrix products, expert_sum(): up_part = jnp.dot(inputs, up_matrix, preferred_element_type=jnp.float32)  11 us
    reshape x1, local copies, waits for them, and re-layouts, on_device(): returned.reshape(slot_total, model_width)  9.66 us
    reshape x1, local copies, waits for them, and re-layouts, on_device(): received.reshape(-1, model_width)  9.66 us
    reshape x1, local copies, waits for them, and re-layouts, on_device(): results = results.astype(jnp.bfloat16).reshape(received.shape)  9.63 us
  transfers between devices with their start and end apart: 4, of which 2 were waited for; matrix products, arithmetic and copies ran while one was open for 21% of the time, Pallas kernels for 0%

commit v1 on v0

v1 whole, which is shorter than its diff:
```python
import functools

import jax
import jax.numpy as jnp
from jax import lax
from jax.experimental import pallas as pl
from jax.experimental.pallas import tpu as pltpu
from jax.sharding import PartitionSpec as P

MESH = pl.DeviceIdType.MESH
BF16 = jnp.bfloat16
F32 = jnp.float32

D = 3584
H = 1024
TOP = 8
TOK = 64
NODES = 16
LOCALS = 8
GROUP = TOK * LOCALS
SLOT = 48
ROWS = NODES * SLOT
COLS = 512
CHUNKS = D // COLS
HALF = GROUP // 2
SHARE = 128
ROW_TILE = 256


def dot(a, b):
    return jnp.dot(a, b, preferred_element_type=F32)


def silu_mul(gate, up):
    return gate / (1.0 + jnp.exp(-gate)) * up


def kernel(
    tokens, ids, weights, eg, eu, ed, sg, su, sd, out,
    held, out1, in1, in2, acc_g, acc_u, hidden, wg, wu, wd, ws, wsd, acc_s, hid_s,
    pick, mix, meta, meta_all, from_sib, from_x,
    load_sem, own_sem, meta_s, meta_r, ag_s, ag_r, fw_s, fw_r, d_s, d_r, c_s, c_r, rs_s, rs_r, rx_s, rx_r,
):
    node = lax.axis_index("node")
    local = lax.axis_index("local")
    z, y, x, core = node // 4, node % 4, local // 2, local % 2
    sib = (node, 2 * x + (1 - core))

    def far(j):
        return ((z + j // 4) % 4) * 4 + (y + j % 4) % 4

    def side(k):
        return (node, 2 * ((x + k) % 4) + core)

    def mate(k):
        return (node, (local + k) % LOCALS)

    def columns(c):
        return pl.ds(pl.multiple_of(c * COLS, COLS), COLS)

    barrier = pltpu.get_barrier_semaphore()
    for j in range(1, NODES):
        pl.semaphore_signal(barrier, inc=1, device_id=(far(j), local), device_id_type=MESH)
    for k in range(1, LOCALS):
        pl.semaphore_signal(barrier, inc=1, device_id=mate(k), device_id_type=MESH)

    loads = [
        pltpu.make_async_copy(sg, ws.at[:, pl.ds(0, SHARE)], load_sem.at[0]),
        pltpu.make_async_copy(su, ws.at[:, pl.ds(SHARE, SHARE)], load_sem.at[1]),
        pltpu.make_async_copy(eg.at[0], wg, load_sem.at[2]),
        pltpu.make_async_copy(eu.at[0], wu, load_sem.at[3]),
        pltpu.make_async_copy(ed.at[0], wd, load_sem.at[4]),
        pltpu.make_async_copy(sd, wsd, load_sem.at[5]),
    ]

    def own_rows():
        return pl.ds(pl.multiple_of(x * TOK, TOK), TOK)

    def own_copy(c):
        return pltpu.make_async_copy(tokens.at[:, columns(c)], held.at[c, core, own_rows()], own_sem.at[c])

    for c in range(CHUNKS):
        own_copy(c).start()
    for load in loads:
        load.start()

    meta[...] = jnp.zeros_like(meta)
    meta[:, 0:TOP] = ids[...].astype(F32)
    meta[:, TOP : 2 * TOP] = weights[...].astype(F32)

    pl.semaphore_wait(barrier, NODES - 1 + LOCALS - 1)

    def meta_copy(k):
        return pltpu.make_async_remote_copy(
            src_ref=meta, dst_ref=meta_all.at[core * 4 + x], send_sem=meta_s.at[k], recv_sem=meta_r.at[k],
            device_id=mate(k), device_id_type=MESH,
        )

    def gather_copy(c, k):
        return pltpu.make_async_remote_copy(
            src_ref=tokens.at[:, columns(c)], dst_ref=held.at[c, core, own_rows()],
            send_sem=ag_s.at[c, k], recv_sem=ag_r.at[c, k], device_id=side(k), device_id_type=MESH,
        )

    def forward_copy(c):
        return pltpu.make_async_remote_copy(
            src_ref=held.at[c, core], dst_ref=held.at[c, core], send_sem=fw_s.at[c], recv_sem=fw_r.at[c],
            device_id=sib, device_id_type=MESH,
        )

    for k in range(1, LOCALS):
        meta_copy(k).start()

    @pl.loop(0, CHUNKS)
    def _(c):
        for k in (1, 3, 2):
            gather_copy(c, k).start()

    meta_all[core * 4 + x] = meta[...]
    acc_s[...] = jnp.zeros_like(acc_s)
    acc_g[...] = jnp.zeros_like(acc_g)
    acc_u[...] = jnp.zeros_like(acc_u)
    for k in range(1, LOCALS):
        meta_copy(k).wait()

    table = jnp.transpose(meta_all[...].reshape(GROUP, 128))
    expert = lax.broadcasted_iota(jnp.int32, (NODES, GROUP), 0) * LOCALS + local
    expert = expert.astype(F32)
    chosen = jnp.zeros((NODES, GROUP), F32)
    gain = jnp.zeros((NODES, GROUP), F32)
    for k in range(TOP):
        hit = jnp.where(table[k : k + 1] == expert, 1.0, 0.0)
        chosen = chosen + hit
        gain = gain + hit * table[TOP + k : TOP + k + 1]
    earlier = lax.broadcasted_iota(jnp.int32, (GROUP, GROUP), 0) < lax.broadcasted_iota(jnp.int32, (GROUP, GROUP), 1)
    rank = dot(chosen.astype(BF16), jnp.where(earlier, 1.0, 0.0).astype(BF16))
    rank = jnp.where(chosen > 0.5, rank, -1.0)
    place = lax.broadcasted_iota(jnp.int32, (SLOT, GROUP), 0).astype(F32)
    for n in range(NODES):
        hit = jnp.where(rank[n : n + 1] == place, 1.0, 0.0)
        pick[n * SLOT : (n + 1) * SLOT] = hit.astype(BF16)

    def rows_copy(src, dst, send, recv, c, j):
        there = far(j)
        return pltpu.make_async_remote_copy(
            src_ref=src.at[c, pl.ds(pl.multiple_of(there * SLOT, SLOT), SLOT)],
            dst_ref=dst.at[c, pl.ds(pl.multiple_of(node * SLOT, SLOT), SLOT)],
            send_sem=send.at[c, j], recv_sem=recv.at[c, j], device_id=(there, local), device_id_type=MESH,
        )

    mine = pl.ds(pl.multiple_of(node * SLOT, SLOT), SLOT)
    loads[0].wait()
    loads[1].wait()

    @pl.loop(0, CHUNKS)
    def _(c):
        for k in (1, 3, 2):
            gather_copy(c, k).wait_recv()
        own_copy(c).wait()
        forward_copy(c).start()
        forward_copy(c).wait_recv()
        block = held[c].reshape(GROUP, COLS)
        out1[c] = dot(pick[...], block).astype(BF16)
        for j in range(1, NODES):
            rows_copy(out1, in1, d_s, d_r, c, j).start()
        in1[c, mine] = out1[c, mine]
        acc_s[...] += dot(block, ws[pl.ds(pl.multiple_of(c * COLS, COLS), COLS), :])

    hid_s[...] = silu_mul(acc_s[:, :SHARE], acc_s[:, SHARE:]).astype(BF16)
    for n in range(NODES):
        hit = jnp.where(rank[n : n + 1] == place, gain[n : n + 1], 0.0)
        mix[:, n * SLOT : (n + 1) * SLOT] = jnp.transpose(hit).astype(BF16)
    for load in loads[2:]:
        load.wait()

    @pl.loop(0, CHUNKS)
    def _(c):
        for j in range(1, NODES):
            rows_copy(out1, in1, d_s, d_r, c, j).wait_recv()
        depth = pl.ds(pl.multiple_of(c * COLS, COLS), COLS)
        for m in range(0, ROWS, ROW_TILE):
            acc_g[m : m + ROW_TILE] += dot(in1[c, m : m + ROW_TILE], wg[depth, :])
            acc_u[m : m + ROW_TILE] += dot(in1[c, m : m + ROW_TILE], wu[depth, :])

    for m in range(0, ROWS, ROW_TILE):
        hidden[m : m + ROW_TILE] = silu_mul(acc_g[m : m + ROW_TILE], acc_u[m : m + ROW_TILE]).astype(BF16)

    @pl.loop(0, CHUNKS)
    def _(c):
        for j in range(1, NODES):
            rows_copy(out1, in1, d_s, d_r, c, j).wait_send()
        out1[c] = dot(hidden[...], wd[:, columns(c)]).astype(BF16)
        for j in range(1, NODES):
            rows_copy(out1, in2, c_s, c_r, c, j).start()
        in2[c, mine] = out1[c, mine]
        for k in (1, 3, 2):
            gather_copy(c, k).wait_send()
        forward_copy(c).wait_send()

    def sib_copy(c):
        return pltpu.make_async_remote_copy(
            src_ref=held.at[c, 1 - core], dst_ref=from_sib.at[c], send_sem=rs_s.at[c], recv_sem=rs_r.at[c],
            device_id=sib, device_id_type=MESH,
        )

    def reduce_copy(c, k):
        return pltpu.make_async_remote_copy(
            src_ref=held.at[c, core, pl.ds(pl.multiple_of((x + k) % 4 * TOK, TOK), TOK)], dst_ref=from_x.at[c, k],
            send_sem=rx_s.at[c, k], recv_sem=rx_r.at[c, k], device_id=side(k), device_id_type=MESH,
        )

    @pl.loop(0, CHUNKS)
    def _(c):
        for j in range(1, NODES):
            rows_copy(out1, in2, c_s, c_r, c, j).wait_recv()
        part = dot(mix[...], in2[c]) + dot(hid_s[...], wsd[:, columns(c)])
        held[c] = part.astype(BF16).reshape(2, HALF, COLS)
        sib_copy(c).start()
        sib_copy(c).wait_recv()
        held[c, core] = (held[c, core].astype(F32) + from_sib[c].astype(F32)).astype(BF16)
        for k in (1, 3, 2):
            reduce_copy(c, k).start()
        total = held[c, core, own_rows()].astype(F32)
        for k in (1, 3, 2):
            reduce_copy(c, k).wait_recv()
            total = total + from_x[c, k].astype(F32)
        out[:, columns(c)] = total.astype(BF16)

    @pl.loop(0, CHUNKS)
    def _(c):
        for j in range(1, NODES):
            rows_copy(out1, in2, c_s, c_r, c, j).wait_send()
        sib_copy(c).wait_send()
        for k in (1, 3, 2):
            reduce_copy(c, k).wait_send()


def on_device(*arrays):
    vmem = pl.BlockSpec(memory_space=pltpu.VMEM)
    hbm = pl.BlockSpec(memory_space=pl.ANY)
    dma = pltpu.SemaphoreType.DMA
    return pl.pallas_call(
        kernel,
        out_shape=jax.ShapeDtypeStruct((TOK, D), BF16),
        in_specs=[hbm, vmem, vmem] + [hbm] * 6,
        out_specs=vmem,
        scratch_shapes=[
            pltpu.VMEM((CHUNKS, 2, HALF, COLS), BF16),
            pltpu.VMEM((CHUNKS, ROWS, COLS), BF16),
            pltpu.VMEM((CHUNKS, ROWS, COLS), BF16),
            pltpu.VMEM((CHUNKS, ROWS, COLS), BF16),
            pltpu.VMEM((ROWS, H), F32),
            pltpu.VMEM((ROWS, H), F32),
            pltpu.VMEM((ROWS, H), BF16),
            pltpu.VMEM((D, H), BF16),
            pltpu.VMEM((D, H), BF16),
            pltpu.VMEM((H, D), BF16),
            pltpu.VMEM((D, 2 * SHARE), BF16),
            pltpu.VMEM((SHARE, D), BF16),
            pltpu.VMEM((GROUP, 2 * SHARE), F32),
            pltpu.VMEM((GROUP, SHARE), BF16),
            pltpu.VMEM((ROWS, GROUP), BF16),
            pltpu.VMEM((GROUP, ROWS), BF16),
            pltpu.VMEM((TOK, 128), F32),
            pltpu.VMEM((LOCALS, TOK, 128), F32),
            pltpu.VMEM((CHUNKS, HALF, COLS), BF16),
            pltpu.VMEM((CHUNKS, 4, TOK, COLS), BF16),
            dma((6,)),
            dma((CHUNKS,)),
            dma((LOCALS,)),
            dma((LOCALS,)),
            dma((CHUNKS, 4)),
            dma((CHUNKS, 4)),
            dma((CHUNKS,)),
            dma((CHUNKS,)),
            dma((CHUNKS, NODES)),
            dma((CHUNKS, NODES)),
            dma((CHUNKS, NODES)),
            dma((CHUNKS, NODES)),
            dma((CHUNKS,)),
            dma((CHUNKS,)),
            dma((CHUNKS, 4)),
            dma((CHUNKS, 4)),
        ],
        compiler_params=pltpu.CompilerParams(
            collective_id=0, has_side_effects=True, vmem_limit_bytes=63 * 2**20
        ),
        cost_estimate=pl.CostEstimate(flops=26 * 10**9, bytes_accessed=26 * 10**6, transcendentals=10**6),
        name="moe",
    )(*arrays)


def solution(mesh):
    both = ("node", "local")
    in_specs = (
        P(both, None),
        P(both, None),
        P(both, None),
        P(both, None, None),
        P(both, None, None),
        P(both, None, None),
        P(None, "local"),
        P(None, "local"),
        P("local", None),
    )
    return jax.shard_map(on_device, mesh=mesh, in_specs=in_specs, out_specs=P(both, None), check_vma=False)
```

time: 316 us -> 178 us (0.56)
  the two profiles are of different devices: /device:TPU:9 before, /device:TPU:31 now
where the time goes in v1:
time: 178 us; the launch traced here: 177 us
  Pallas kernels  173 us (97%)
  local copies, waits for them, and re-layouts  4.57 us (3%)
    pallas_call x1, Pallas kernels, on_device(): pl.pallas_call(kernel, out_shape=jax.ShapeDtypeStruct((TOK, D), BF16), in...  173 us
    unnamed x3, local copies, waits for them, and re-layouts  4.57 us

profile of v1, /device:TPU:31, one launch (start us, length us, event | category | flops | bytes accessed | tf_op | source)
XLA Modules:
  0.0 177.4 jit_solution(7209839448395235869)
XLA Ops:
  0.0 1.4 copy.11.weights
  1.4 1.4 copy.10.ids
  2.8 172.8 %moe.1 = bf16[64,3584]{1,0:T(8,128)(2,1)} custom-call(bf16[64,3584]{1,0:T(8,128)(2,1)} %tokens.1, s32[64,8]{1,0:T(8,128)} %copy.10.ids, bf16[64,8]{1,0:T(8,128)(2,1)} %copy.11.weights, bf16[1,3584,1024]{2,1,0:T(8,128)(2,1)} %eg.1, bf16[1,3584,1024]{2,1,0:T(8,128)(2,1)} %eu.1, bf16[1,1024,3584]{2,1,0:T(8,128)(2,1)} %ed.1, bf16[3584,128]{1,0:T(8,128)(2,1)} %sg.1, ...), custom_call_target="tpu_custom_call" | custom-call | flops 25999998976 | bytes 26000000 | tf_op jit(solution)/shard_map/moe/pallas_call | solution.py:242
  175.6 1.8 %copy.13 = bf16[64,3584]{1,0:T(8,128)(2,1)} copy(bf16[64,3584]{1,0:T(8,128)(2,1)} %moe.1) | data formatting | bytes 917504

commit v2 on v1

v2 whole, which is shorter than its diff:
```python
import jax
import jax.numpy as jnp
from jax import lax
from jax.experimental import pallas as pl
from jax.experimental.pallas import tpu as pltpu
from jax.sharding import PartitionSpec as P

MESH = pl.DeviceIdType.MESH
BF16 = jnp.bfloat16
F32 = jnp.float32

D = 3584
H = 1024
TOP = 8
TOK = 64
NODES = 16
LOCALS = 8
GROUP = TOK * LOCALS
PAIR = 2 * TOK
SLOT = 48
PART = 12
BAND = NODES * PART
ROWS = NODES * SLOT
SPREAD = LOCALS * BAND
COLS = 512
WIDE = COLS // 2
CHUNKS = D // COLS
ONCE = 3
DIRECT = CHUNKS - ONCE
HALF = GROUP // 2
SHARE = 128
ROW_TILE = 256
SLOTS = 3


def dot(a, b):
    return jnp.dot(a, b, preferred_element_type=F32)


def silu_mul(gate, up):
    return gate / (1.0 + jnp.exp(-gate)) * up


def count(shape, dim):
    return lax.broadcasted_iota(jnp.int32, shape, dim).astype(F32)


def quotient(values, by):
    return jnp.floor((values + 0.5) * (1.0 / by))


def ones_where(condition):
    return jnp.where(condition, 1.0, 0.0)


def kernel(
    tokens, ids, weights, eg, eu, ed, sg, su, sd, out,
    held, out1, in1, in2, ao, ai, ae, xo, xi, xe, acc_g, acc_u, hidden, hidden_a, wgu, wds, ws, wsd, acc_s, hid_s,
    pick, mix, pick_a, mix_a, spread, merge, square, work, meta, meta_all, slots_out, slots_in, from_sib, from_x,
    load_sem, gu_sem, wd_sem, own_sem, meta_s, meta_r, sm_s, sm_r, ag_s, ag_r, fw_s, fw_r,
    d_s, d_r, c_s, c_r, ad_s, ad_r, ac_s, ac_r, xd_s, xd_r, xc_s, xc_r, rs_s, rs_r, rx_s, rx_r,
):
    node = lax.axis_index("node")
    local = lax.axis_index("local")
    z, y, x, core = node // 4, node % 4, local // 2, local % 2
    sib = (node, 2 * x + (1 - core))

    def far(j):
        return ((z + j // 4) % 4) * 4 + (y + j % 4) % 4

    def side(k):
        return (node, 2 * ((x + k) % 4) + core)

    def mate(k):
        return (local + k) % LOCALS

    def block(i, size):
        return pl.ds(pl.multiple_of(i * size, size), size)

    def columns(c):
        return block(c, COLS)

    def tok_rows(i):
        return block(i, TOK)

    def remote(src, dst, send, recv, device):
        return pltpu.make_async_remote_copy(
            src_ref=src, dst_ref=dst, send_sem=send, recv_sem=recv, device_id=device, device_id_type=MESH
        )

    barrier = pltpu.get_barrier_semaphore()
    for j in range(1, NODES):
        pl.semaphore_signal(barrier, inc=1, device_id=(far(j), local), device_id_type=MESH)
    for k in range(1, LOCALS):
        pl.semaphore_signal(barrier, inc=1, device_id=(node, mate(k)), device_id_type=MESH)

    loads = [
        pltpu.make_async_copy(sg, ws.at[:, pl.ds(0, SHARE)], load_sem.at[0]),
        pltpu.make_async_copy(su, ws.at[:, pl.ds(SHARE, SHARE)], load_sem.at[1]),
        pltpu.make_async_copy(sd, wsd, load_sem.at[2]),
    ]

    def own_copy(c):
        return pltpu.make_async_copy(tokens.at[:, columns(c)], held.at[c, core, tok_rows(x)], own_sem.at[c])

    def gate_load(c, s):
        return pltpu.make_async_copy(eg.at[0, columns(c)], wgu.at[s, 0], gu_sem.at[s, 0])

    def up_load(c, s):
        return pltpu.make_async_copy(eu.at[0, columns(c)], wgu.at[s, 1], gu_sem.at[s, 1])

    def down_load(c, s):
        return pltpu.make_async_copy(ed.at[0, :, columns(c)], wds.at[s], wd_sem.at[s])

    def in_turn(q):
        return (1 - q % 2) * ONCE + q // 2

    for c in range(CHUNKS):
        own_copy(c).start()

    meta[...] = jnp.zeros_like(meta)
    meta[0:TOP, 0:TOK] = ids[...].astype(F32) + 1.0
    meta[TOP : 2 * TOP, 0:TOK] = weights[...].astype(F32)

    pl.semaphore_wait(barrier, NODES - 1 + LOCALS - 1)

    def meta_copy(k):
        return remote(meta, meta_all.at[core * 4 + x], meta_s.at[k], meta_r.at[k], (node, mate(k)))

    def gather_copy(c, k):
        return remote(tokens.at[:, columns(c)], held.at[c, core, tok_rows(x)], ag_s.at[c, k], ag_r.at[c, k], side(k))

    def forward_copy(c, k):
        mid = held.at[c, core, tok_rows((x + 4 - k) % 4)]
        return remote(tokens.at[:, columns(c)] if k == 0 else mid, mid, fw_s.at[c, k], fw_r.at[c, k], sib)

    for k in range(1, LOCALS):
        meta_copy(k).start()
    for c in range(CHUNKS):
        forward_copy(c, 0).start()

    @pl.loop(ONCE, CHUNKS)
    def _(c):
        for k in (1, 3, 2):
            gather_copy(c, k).start()

    for load in loads:
        load.start()
    for s in range(SLOTS):
        gate_load(in_turn(s), s).start()
        up_load(in_turn(s), s).start()
        down_load(s, s).start()
    meta_all[core * 4 + x] = meta[...]
    slots_out[...] = jnp.zeros_like(slots_out)
    for k in range(1, LOCALS):
        meta_copy(k).wait()

    chip_table = jnp.concatenate([meta_all[x][:, :TOK], meta_all[4 + x][:, :TOK]], axis=1)
    chip_node = quotient(chip_table[:TOP] - 1.0, LOCALS)
    node_row = count((NODES, PAIR), 0)
    chosen = jnp.zeros((NODES, PAIR), F32)
    for k in range(0, TOP, 2):
        chosen = chosen + ones_where(chip_node[k : k + 1] == node_row)
    earlier = count((PAIR, PAIR), 0) < count((PAIR, PAIR), 1)
    rank_a = dot(chosen.astype(BF16), ones_where(earlier).astype(BF16))
    rank_a = jnp.where(chosen > 0.5, rank_a, -1.0)
    place_a = count((SLOT, PAIR), 0)
    for n in range(NODES):
        pick_a[n * SLOT : (n + 1) * SLOT] = ones_where(rank_a[n : n + 1] == place_a).astype(BF16)
    notes = lax.dot_general(
        chip_table.astype(BF16), pick_a[...], (((1,), (1,)), ((), ())), preferred_element_type=F32
    )
    for n in range(NODES):
        slots_out[n, :, 0:SLOT] = notes[:, n * SLOT : (n + 1) * SLOT]

    def notes_copy(j):
        there = far(j)
        return remote(slots_out.at[there], slots_in.at[node], sm_s.at[j], sm_r.at[j], (there, local))

    def rows_copy(src, dst, send, recv, c, j):
        there = far(j)
        return remote(
            src.at[c, block(there, SLOT)], dst.at[c, block(node, SLOT)], send.at[c, j], recv.at[c, j], (there, local)
        )

    mine = block(node, SLOT)
    wide = block(core, WIDE)

    for j in range(1, NODES):
        notes_copy(j).start()
    slots_in[node] = slots_out[node]

    @pl.loop(0, ONCE)
    def _(a):
        own_copy(a).wait()
        forward_copy(a, 0).wait_recv()
        rows = jnp.concatenate([held[a, 0, tok_rows(x), wide], held[a, 1, tok_rows(x), wide]], axis=0)
        ao[a] = dot(pick_a[...], rows).astype(BF16)
        for j in range(1, NODES):
            rows_copy(ao, ai, ad_s, ad_r, a, j).start()
        ai[a, mine] = ao[a, mine]

    table = jnp.concatenate([meta_all[d][:, :TOK] for d in range(LOCALS)], axis=1)
    expert = count((NODES, GROUP), 0) * LOCALS + (local + 1).astype(F32)
    chosen = jnp.zeros((NODES, GROUP), F32)
    gain = jnp.zeros((NODES, GROUP), F32)
    for k in range(TOP):
        hit = ones_where(table[k : k + 1] == expert)
        chosen = chosen + hit
        gain = gain + hit * table[TOP + k : TOP + k + 1]

    def chip_of(t):
        device = quotient(t, TOK)
        return device - 4.0 * quotient(device, 4)

    first, then = count((GROUP, 1), 0), count((1, GROUP), 1)
    earlier = (first < then) & (chip_of(first) == chip_of(then))
    rank = dot(chosen.astype(BF16), ones_where(earlier).astype(BF16)) + chip_of(then) * PART
    rank = jnp.where(chosen > 0.5, rank, -1.0)
    place = count((SLOT, GROUP), 0)
    for n in range(NODES):
        pick[n * SLOT : (n + 1) * SLOT] = ones_where(rank[n : n + 1] == place).astype(BF16)

    acc_s[...] = jnp.zeros_like(acc_s)
    acc_g[...] = jnp.zeros_like(acc_g)
    acc_u[...] = jnp.zeros_like(acc_u)
    loads[0].wait()
    loads[1].wait()

    def gathered(c):
        for k in (1, 3, 2):
            gather_copy(c, k).wait_recv()
            forward_copy(c, k).start()
        for k in (1, 3, 2):
            forward_copy(c, k).wait_recv()
        return held[c].reshape(GROUP, COLS)

    def direct_rows(b):
        c = b + ONCE
        own_copy(c).wait()
        forward_copy(c, 0).wait_recv()
        rows = gathered(c)
        out1[b] = dot(pick[...], rows).astype(BF16)
        for j in range(1, NODES):
            rows_copy(out1, in1, d_s, d_r, b, j).start()
        in1[b, mine] = out1[b, mine]
        acc_s[...] += dot(rows, ws[columns(c), :])

    def pass_copy(a, k):
        there = mate(k)
        return remote(
            xo.at[a, block(there, BAND)], xi.at[a, block(core * 4 + x, BAND)], xd_s.at[a, k], xd_r.at[a, k], (node, there)
        )

    def pass_rows(a):
        for j in range(1, NODES):
            rows_copy(ao, ai, ad_s, ad_r, a, j).wait_recv()
        xo[a] = dot(spread[...], ai[a]).astype(BF16)
        for k in range(1, LOCALS):
            pass_copy(a, k).start()
        xi[a, block(core * 4 + x, BAND)] = xo[a, block(local, BAND)]

    direct_rows(0)

    for j in range(1, NODES):
        notes_copy(j).wait()
    slot_table = jnp.concatenate([slots_in[n][:, :SLOT] for n in range(NODES)], axis=1)
    expert = count((LOCALS, ROWS), 0) + (node * LOCALS + 1).astype(F32)
    chosen = jnp.zeros((LOCALS, ROWS), F32)
    gain_a = jnp.zeros((LOCALS, ROWS), F32)
    for k in range(TOP):
        hit = ones_where(slot_table[k : k + 1] == expert)
        chosen = chosen + hit
        gain_a = gain_a + hit * slot_table[TOP + k : TOP + k + 1]
    first, then = count((ROWS, 1), 0), count((1, ROWS), 1)
    earlier = (first < then) & (quotient(first, SLOT) == quotient(then, SLOT))
    square[...] = ones_where(earlier).astype(BF16)
    seat = dot(chosen.astype(BF16), square[...]) + quotient(then, SLOT) * PART
    seat = jnp.where(chosen > 0.5, seat, -1.0)
    place_x = count((BAND, ROWS), 0)
    for l in range(LOCALS):
        spread[l * BAND : (l + 1) * BAND] = ones_where(seat[l : l + 1] == place_x).astype(BF16)

    @pl.loop(1, DIRECT)
    def _(b):
        direct_rows(b)
        pass_rows(b - 1)

    @pl.loop(0, ONCE)
    def _(c):
        for k in (1, 3, 2):
            gather_copy(c, k).start()

    row, column = count((ROWS, 1), 0), count((1, ROWS), 1)
    by_node = quotient(row, SLOT)
    by_chip = quotient(row - by_node * SLOT, PART)
    square[...] = ones_where(row - by_node * SLOT - by_chip * PART + by_chip * BAND + by_node * PART == column).astype(BF16)
    for n in range(NODES):
        hit = jnp.where(rank[n : n + 1] == place, gain[n : n + 1], 0.0)
        mix[:, n * SLOT : (n + 1) * SLOT] = jnp.transpose(hit).astype(BF16)
    for n in range(0, NODES, 8):
        hits = [ones_where(rank_a[i : i + 1] == place_a) for i in range(n, n + 8)]
        mix_a[:, n * SLOT : (n + 8) * SLOT] = jnp.transpose(jnp.concatenate(hits, axis=0)).astype(BF16)
    for l in range(0, LOCALS, 2):
        hits = [jnp.where(seat[i : i + 1] == place_x, gain_a[i : i + 1], 0.0) for i in (l, l + 1)]
        merge[:, l * BAND : (l + 2) * BAND] = jnp.transpose(jnp.concatenate(hits, axis=0)).astype(BF16)

    def gate_up(q, get):
        s = q % SLOTS
        gate_load(0, s).wait()
        up_load(0, s).wait()
        for m in range(0, ROWS, ROW_TILE):
            rows = get(m)
            acc_g[m : m + ROW_TILE] += dot(rows, wgu[s, 0])
            acc_u[m : m + ROW_TILE] += dot(rows, wgu[s, 1])

        @pl.when(q + SLOTS < CHUNKS)
        def _():
            gate_load(in_turn(q + SLOTS), s).start()
            up_load(in_turn(q + SLOTS), s).start()

    @pl.loop(0, DIRECT)
    def _(i):
        for j in range(1, NODES):
            rows_copy(out1, in1, d_s, d_r, i, j).wait_recv()
        gate_up(2 * i, lambda m: in1[i, m : m + ROW_TILE])

        @pl.when(i < ONCE)
        def _():
            for k in range(1, LOCALS):
                pass_copy(i, k).wait_recv()
            for h in range(2):
                work[:, h * WIDE : (h + 1) * WIDE] = dot(square[...], xi[i, h * ROWS : (h + 1) * ROWS]).astype(BF16)
            gate_up(2 * i + 1, lambda m: work[m : m + ROW_TILE])
            acc_s[...] += dot(gathered(i), ws[columns(i), :])

    by_chip = quotient(row, BAND)
    by_node = quotient(row - by_chip * BAND, PART)
    square[...] = ones_where(row - by_chip * BAND - by_node * PART + by_node * SLOT + by_chip * PART == column).astype(BF16)
    for m in range(0, ROWS, ROW_TILE):
        hidden[m : m + ROW_TILE] = silu_mul(acc_g[m : m + ROW_TILE], acc_u[m : m + ROW_TILE]).astype(BF16)
    for m in range(0, ROWS, ROW_TILE):
        hidden_a[m : m + ROW_TILE] = dot(square[m : m + ROW_TILE], hidden[...]).astype(BF16)

    def back_copy(a, k):
        there = mate(k)
        return remote(
            xo.at[a, block(there % 2 * 4 + there // 2, BAND)], xe.at[a, block(local, BAND)],
            xc_s.at[a, k], xc_r.at[a, k], (node, there),
        )

    def next_down(c):
        @pl.when(c + SLOTS < CHUNKS)
        def _():
            down_load(c + SLOTS, c % SLOTS).start()

    @pl.loop(0, ONCE)
    def _(a):
        for k in range(1, LOCALS):
            pass_copy(a, k).wait_send()
        s = a % SLOTS
        down_load(0, s).wait()
        for h in range(2):
            xo[a, h * ROWS : (h + 1) * ROWS] = dot(hidden_a[...], wds[s, :, h * WIDE : (h + 1) * WIDE]).astype(BF16)
        next_down(a)
        for k in range(1, LOCALS):
            back_copy(a, k).start()
        xe[a, block(local, BAND)] = xo[a, block(core * 4 + x, BAND)]

    def node_sums(a):
        for j in range(1, NODES):
            rows_copy(ao, ai, ad_s, ad_r, a, j).wait_send()
        for k in range(1, LOCALS):
            back_copy(a, k).wait_recv()
        ao[a] = dot(merge[...], xe[a]).astype(BF16)
        for j in range(1, NODES):
            rows_copy(ao, ae, ac_s, ac_r, a, j).start()
        ae[a, mine] = ao[a, mine]

    @pl.loop(0, DIRECT)
    def _(b):
        for j in range(1, NODES):
            rows_copy(out1, in1, d_s, d_r, b, j).wait_send()
        c = b + ONCE
        s = c % SLOTS
        down_load(0, s).wait()
        out1[b] = dot(hidden[...], wds[s]).astype(BF16)
        next_down(c)
        for j in range(1, NODES):
            rows_copy(out1, in2, c_s, c_r, b, j).start()
        in2[b, mine] = out1[b, mine]

        @pl.when(b >= 1)
        def _():
            node_sums(b - 1)

    hid_s[...] = silu_mul(acc_s[:, :SHARE], acc_s[:, SHARE:]).astype(BF16)
    loads[2].wait()

    def sib_copy(c):
        return remote(held.at[c, 1 - core], from_sib.at[c], rs_s.at[c], rs_r.at[c], sib)

    def reduce_copy(c, k):
        return remote(
            held.at[c, core, tok_rows((x + k) % 4)], from_x.at[c, k], rx_s.at[c, k], rx_r.at[c, k], side(k)
        )

    def shared_part(c):
        for k in (1, 3, 2):
            gather_copy(c, k).wait_send()
        for k in range(4):
            forward_copy(c, k).wait_send()
        return dot(hid_s[...], wsd[:, columns(c)])

    def reduce(c):
        sib_copy(c).start()
        sib_copy(c).wait_recv()
        held[c, core] = (held[c, core].astype(F32) + from_sib[c].astype(F32)).astype(BF16)
        for k in (1, 3, 2):
            reduce_copy(c, k).start()

    def finish(c):
        total = held[c, core, tok_rows(x)].astype(F32)
        for k in (1, 3, 2):
            reduce_copy(c, k).wait_recv()
            total = total + from_x[c, k].astype(F32)
        out[:, columns(c)] = total.astype(BF16)

    @pl.loop(0, DIRECT)
    def _(i):
        for j in range(1, NODES):
            rows_copy(out1, in2, c_s, c_r, i, j).wait_recv()
        c = i + ONCE
        part = dot(mix[...], in2[i]) + shared_part(c)
        held[c] = part.astype(BF16).reshape(2, HALF, COLS)
        reduce(c)

        @pl.when(i >= 2)
        def _():
            finish(i - 2)

        @pl.when(i >= 1)
        def _():
            a = i - 1
            for j in range(1, NODES):
                rows_copy(ao, ae, ac_s, ac_r, a, j).wait_recv()
            held[a] = shared_part(a).astype(BF16).reshape(2, HALF, COLS)
            sums = dot(mix_a[...], ae[a])
            for h in range(2):
                old = held[a, h, tok_rows(x), wide].astype(F32)
                held[a, h, tok_rows(x), wide] = (old + sums[h * TOK : (h + 1) * TOK]).astype(BF16)
            reduce(a)

        finish(c)

    finish(ONCE - 1)

    @pl.loop(0, DIRECT)
    def _(b):
        for j in range(1, NODES):
            rows_copy(out1, in2, c_s, c_r, b, j).wait_send()

    @pl.loop(0, ONCE)
    def _(a):
        for k in range(1, LOCALS):
            back_copy(a, k).wait_send()
        for j in range(1, NODES):
            rows_copy(ao, ae, ac_s, ac_r, a, j).wait_send()

    @pl.loop(0, CHUNKS)
    def _(c):
        sib_copy(c).wait_send()
        for k in (1, 3, 2):
            reduce_copy(c, k).wait_send()


def on_device(tokens, ids, weights, *matrices):
    vmem = pl.BlockSpec(memory_space=pltpu.VMEM)
    hbm = pl.BlockSpec(memory_space=pl.ANY)
    dma = pltpu.SemaphoreType.DMA
    return pl.pallas_call(
        kernel,
        out_shape=jax.ShapeDtypeStruct((TOK, D), BF16),
        in_specs=[hbm, vmem, vmem] + [hbm] * 6,
        out_specs=vmem,
        scratch_shapes=[
            pltpu.VMEM((CHUNKS, 2, HALF, COLS), BF16),
            pltpu.VMEM((DIRECT, ROWS, COLS), BF16),
            pltpu.VMEM((DIRECT, ROWS, COLS), BF16),
            pltpu.VMEM((DIRECT, ROWS, COLS), BF16),
            pltpu.VMEM((ONCE, ROWS, WIDE), BF16),
            pltpu.VMEM((ONCE, ROWS, WIDE), BF16),
            pltpu.VMEM((ONCE, ROWS, WIDE), BF16),
            pltpu.VMEM((ONCE, SPREAD, WIDE), BF16),
            pltpu.VMEM((ONCE, SPREAD, WIDE), BF16),
            pltpu.VMEM((ONCE, SPREAD, WIDE), BF16),
            pltpu.VMEM((ROWS, H), F32),
            pltpu.VMEM((ROWS, H), F32),
            pltpu.VMEM((ROWS, H), BF16),
            pltpu.VMEM((ROWS, H), BF16),
            pltpu.VMEM((SLOTS, 2, COLS, H), BF16),
            pltpu.VMEM((SLOTS, H, COLS), BF16),
            pltpu.VMEM((D, 2 * SHARE), BF16),
            pltpu.VMEM((SHARE, D), BF16),
            pltpu.VMEM((GROUP, 2 * SHARE), F32),
            pltpu.VMEM((GROUP, SHARE), BF16),
            pltpu.VMEM((ROWS, GROUP), BF16),
            pltpu.VMEM((GROUP, ROWS), BF16),
            pltpu.VMEM((ROWS, PAIR), BF16),
            pltpu.VMEM((PAIR, ROWS), BF16),
            pltpu.VMEM((SPREAD, ROWS), BF16),
            pltpu.VMEM((ROWS, SPREAD), BF16),
            pltpu.VMEM((ROWS, ROWS), BF16),
            pltpu.VMEM((ROWS, COLS), BF16),
            pltpu.VMEM((2 * TOP, 128), F32),
            pltpu.VMEM((LOCALS, 2 * TOP, 128), F32),
            pltpu.VMEM((NODES, 2 * TOP, 128), F32),
            pltpu.VMEM((NODES, 2 * TOP, 128), F32),
            pltpu.VMEM((CHUNKS, HALF, COLS), BF16),
            pltpu.VMEM((CHUNKS, 4, TOK, COLS), BF16),
            dma((3,)),
            dma((SLOTS, 2)),
            dma((SLOTS,)),
            dma((CHUNKS,)),
            dma((LOCALS,)),
            dma((LOCALS,)),
            dma((NODES,)),
            dma((NODES,)),
            dma((CHUNKS, 4)),
            dma((CHUNKS, 4)),
            dma((CHUNKS, 4)),
            dma((CHUNKS, 4)),
            dma((DIRECT, NODES)),
            dma((DIRECT, NODES)),
            dma((DIRECT, NODES)),
            dma((DIRECT, NODES)),
            dma((ONCE, NODES)),
            dma((ONCE, NODES)),
            dma((ONCE, NODES)),
            dma((ONCE, NODES)),
            dma((ONCE, LOCALS)),
            dma((ONCE, LOCALS)),
            dma((ONCE, LOCALS)),
            dma((ONCE, LOCALS)),
            dma((CHUNKS,)),
            dma((CHUNKS,)),
            dma((CHUNKS, 4)),
            dma((CHUNKS, 4)),
        ],
        compiler_params=pltpu.CompilerParams(
            collective_id=0, has_side_effects=True, vmem_limit_bytes=63 * 2**20
        ),
        cost_estimate=pl.CostEstimate(flops=32 * 10**9, bytes_accessed=26 * 10**6, transcendentals=10**6),
        name="moe",
    )(tokens, ids.T, weights.T, *matrices)


def solution(mesh):
    both = ("node", "local")
    in_specs = (
        P(both, None),
        P(both, None),
        P(both, None),
        P(both, None, None),
        P(both, None, None),
        P(both, None, None),
        P(None, "local"),
        P(None, "local"),
        P("local", None),
    )
    return jax.shard_map(on_device, mesh=mesh, in_specs=in_specs, out_specs=P(both, None), check_vma=False)
```

time: 178 us -> 151 us (0.85)
  the two profiles are of different devices: /device:TPU:31 before, /device:TPU:9 now
where the time goes in v2:
time: 151 us; the launch traced here: 150 us
  Pallas kernels  149 us (99%)
  local copies, waits for them, and re-layouts  1.82 us (1%)
    pallas_call x1, Pallas kernels, on_device(): pl.pallas_call(kernel, out_shape=jax.ShapeDtypeStruct((TOK, D), BF16), in...  149 us

profile of v2, /device:TPU:9, one launch (start us, length us, event | category | flops | bytes accessed | tf_op | source)
XLA Modules:
  0.0 150.4 jit_solution(1331709359655205366)
XLA Ops:
  0.0 148.6 %moe.1 = bf16[64,3584]{1,0:T(8,128)(2,1)} custom-call(bf16[64,3584]{1,0:T(8,128)(2,1)} %tokens.1, s32[8,64]{1,0:T(8,128)} %bitcast.2, bf16[8,64]{1,0:T(8,128)(2,1)} %bitcast.3, bf16[1,3584,1024]{2,1,0:T(8,128)(2,1)} %eg.1, bf16[1,3584,1024]{2,1,0:T(8,128)(2,1)} %eu.1, bf16[1,1024,3584]{2,1,0:T(8,128)(2,1)} %ed.1, bf16[3584,128]{1,0:T(8,128)(2,1)} %sg.1, ...), custom_call_target="tpu_custom_call" | custom-call | flops 32000000000 | bytes 26000000 | tf_op jit(solution)/shard_map/moe/pallas_call | solution.py:481
  148.6 1.8 %copy.11 = bf16[64,3584]{1,0:T(8,128)(2,1)} copy(bf16[64,3584]{1,0:T(8,128)(2,1)} %moe.1) | data formatting | bytes 917504

commit v3 on v2

--- a/solution.py
+++ b/solution.py
@@ -56,9 +56,9 @@
 def kernel(
     tokens, ids, weights, eg, eu, ed, sg, su, sd, out,
     held, out1, in1, in2, ao, ai, ae, xo, xi, xe, acc_g, acc_u, hidden, hidden_a, wgu, wds, ws, wsd, acc_s, hid_s,
-    pick, mix, pick_a, mix_a, spread, merge, square, work, meta, meta_all, slots_out, slots_in, from_sib, from_x,
+    pick, mix, pick_a, mix_a, spread, merge, square, work, meta, meta_all, slots_out, slots_in, from_sib, from_x, extra_out, extra,
     load_sem, gu_sem, wd_sem, own_sem, meta_s, meta_r, sm_s, sm_r, ag_s, ag_r, fw_s, fw_r,
-    d_s, d_r, c_s, c_r, ad_s, ad_r, ac_s, ac_r, xd_s, xd_r, xc_s, xc_r, rs_s, rs_r, rx_s, rx_r,
+    d_s, d_r, c_s, c_r, ad_s, ad_r, ac_s, ac_r, xd_s, xd_r, xc_s, xc_r, rs_s, rs_r, rx_s, rx_r, ex_s, ex_r,
 ):
     node = lax.axis_index("node")
     local = lax.axis_index("local")
@@ -113,7 +113,7 @@
         return pltpu.make_async_copy(ed.at[0, :, columns(c)], wds.at[s], wd_sem.at[s])
 
     def in_turn(q):
-        return (1 - q % 2) * ONCE + q // 2
+        return (q % 2 + q // (2 * ONCE)) * ONCE + q // 2
 
     for c in range(CHUNKS):
         own_copy(c).start()
@@ -121,37 +121,46 @@
     meta[...] = jnp.zeros_like(meta)
     meta[0:TOP, 0:TOK] = ids[...].astype(F32) + 1.0
     meta[TOP : 2 * TOP, 0:TOK] = weights[...].astype(F32)
-
-    pl.semaphore_wait(barrier, NODES - 1 + LOCALS - 1)
-
-    def meta_copy(k):
-        return remote(meta, meta_all.at[core * 4 + x], meta_s.at[k], meta_r.at[k], (node, mate(k)))
-
-    def gather_copy(c, k):
-        return remote(tokens.at[:, columns(c)], held.at[c, core, tok_rows(x)], ag_s.at[c, k], ag_r.at[c, k], side(k))
-
-    def forward_copy(c, k):
-        mid = held.at[c, core, tok_rows((x + 4 - k) % 4)]
-        return remote(tokens.at[:, columns(c)] if k == 0 else mid, mid, fw_s.at[c, k], fw_r.at[c, k], sib)
-
-    for k in range(1, LOCALS):
-        meta_copy(k).start()
-    for c in range(CHUNKS):
-        forward_copy(c, 0).start()
-
-    @pl.loop(ONCE, CHUNKS)
-    def _(c):
-        for k in (1, 3, 2):
-            gather_copy(c, k).start()
 
     for load in loads:
         load.start()
     for s in range(SLOTS):
         gate_load(in_turn(s), s).start()
         up_load(in_turn(s), s).start()
-        down_load(s, s).start()
+    for s, c in enumerate((ONCE, 0, 1)):
+        down_load(c, s).start()
+
+    slots_out[...] = jnp.zeros_like(slots_out)
+    acc_s[...] = jnp.zeros_like(acc_s)
+    acc_g[...] = jnp.zeros_like(acc_g)
+    acc_u[...] = jnp.zeros_like(acc_u)
+    first, then = count((ROWS, 1), 0), count((1, ROWS), 1)
+    earlier = (first < then) & (quotient(first, SLOT) == quotient(then, SLOT))
+    square[...] = ones_where(earlier).astype(BF16)
+
+    pl.semaphore_wait(barrier, NODES - 1 + LOCALS - 1)
+
+    def meta_copy(k):
+        return remote(meta, meta_all.at[core * 4 + x], meta_s.at[k], meta_r.at[k], (node, mate(k)))
+
+    def gather_copy(c, k):
+        return remote(tokens.at[:, columns(c)], held.at[c, core, tok_rows(x)], ag_s.at[c, k], ag_r.at[c, k], side(k))
+
+    def forward_copy(c, k):
+        mid = held.at[c, core, tok_rows((x + 4 - k) % 4)]
+        return remote(tokens.at[:, columns(c)] if k == 0 else mid, mid, fw_s.at[c, k], fw_r.at[c, k], sib)
+
+    for k in range(1, LOCALS):
+        meta_copy(k).start()
+    for c in range(CHUNKS):
+        forward_copy(c, 0).start()
+
+    @pl.loop(ONCE, CHUNKS)
+    def _(c):
+        for k in (1, 3, 2):
+            gather_copy(c, k).start()
+
     meta_all[core * 4 + x] = meta[...]
-    slots_out[...] = jnp.zeros_like(slots_out)
     for k in range(1, LOCALS):
         meta_copy(k).wait()
 
@@ -221,16 +230,15 @@
     for n in range(NODES):
         pick[n * SLOT : (n + 1) * SLOT] = ones_where(rank[n : n + 1] == place).astype(BF16)
 
-    acc_s[...] = jnp.zeros_like(acc_s)
-    acc_g[...] = jnp.zeros_like(acc_g)
-    acc_u[...] = jnp.zeros_like(acc_u)
     loads[0].wait()
     loads[1].wait()
 
-    def gathered(c):
+    def hand_on(c):
         for k in (1, 3, 2):
             gather_copy(c, k).wait_recv()
             forward_copy(c, k).start()
+
+    def gathered(c):
         for k in (1, 3, 2):
             forward_copy(c, k).wait_recv()
         return held[c].reshape(GROUP, COLS)
@@ -239,6 +247,7 @@
         c = b + ONCE
         own_copy(c).wait()
         forward_copy(c, 0).wait_recv()
+        hand_on(c)
         rows = gathered(c)
         out1[b] = dot(pick[...], rows).astype(BF16)
         for j in range(1, NODES):
@@ -272,19 +281,17 @@
         hit = ones_where(slot_table[k : k + 1] == expert)
         chosen = chosen + hit
         gain_a = gain_a + hit * slot_table[TOP + k : TOP + k + 1]
-    first, then = count((ROWS, 1), 0), count((1, ROWS), 1)
-    earlier = (first < then) & (quotient(first, SLOT) == quotient(then, SLOT))
-    square[...] = ones_where(earlier).astype(BF16)
-    seat = dot(chosen.astype(BF16), square[...]) + quotient(then, SLOT) * PART
+    slot_row = count((1, ROWS), 1)
+    seat = dot(chosen.astype(BF16), square[...]) + quotient(slot_row, SLOT) * PART
     seat = jnp.where(chosen > 0.5, seat, -1.0)
     place_x = count((BAND, ROWS), 0)
     for l in range(LOCALS):
         spread[l * BAND : (l + 1) * BAND] = ones_where(seat[l : l + 1] == place_x).astype(BF16)
 
-    @pl.loop(1, DIRECT)
-    def _(b):
-        direct_rows(b)
-        pass_rows(b - 1)
+    @pl.loop(0, ONCE)
+    def _(a):
+        pass_rows(a)
+        direct_rows(a + 1)
 
     @pl.loop(0, ONCE)
     def _(c):
@@ -319,26 +326,48 @@
             gate_load(in_turn(q + SLOTS), s).start()
             up_load(in_turn(q + SLOTS), s).start()
 
-    @pl.loop(0, DIRECT)
+    @pl.loop(0, ONCE)
     def _(i):
+        for k in range(1, LOCALS):
+            pass_copy(i, k).wait_recv()
+        for h in range(2):
+            work[:, h * WIDE : (h + 1) * WIDE] = dot(square[...], xi[i, h * ROWS : (h + 1) * ROWS]).astype(BF16)
+        gate_up(2 * i, lambda m: work[m : m + ROW_TILE])
         for j in range(1, NODES):
             rows_copy(out1, in1, d_s, d_r, i, j).wait_recv()
-        gate_up(2 * i, lambda m: in1[i, m : m + ROW_TILE])
-
-        @pl.when(i < ONCE)
-        def _():
-            for k in range(1, LOCALS):
-                pass_copy(i, k).wait_recv()
-            for h in range(2):
-                work[:, h * WIDE : (h + 1) * WIDE] = dot(square[...], xi[i, h * ROWS : (h + 1) * ROWS]).astype(BF16)
-            gate_up(2 * i + 1, lambda m: work[m : m + ROW_TILE])
-            acc_s[...] += dot(gathered(i), ws[columns(i), :])
+        gate_up(2 * i + 1, lambda m: in1[i, m : m + ROW_TILE])
 
     by_chip = quotient(row, BAND)
     by_node = quotient(row - by_chip * BAND, PART)
     square[...] = ones_where(row - by_chip * BAND - by_node * PART + by_node * SLOT + by_chip * PART == column).astype(BF16)
-    for m in range(0, ROWS, ROW_TILE):
-        hidden[m : m + ROW_TILE] = silu_mul(acc_g[m : m + ROW_TILE], acc_u[m : m + ROW_TILE]).astype(BF16)
+
+    for j in range(1, NODES):
+        rows_copy(out1, in1, d_s, d_r, 0, j).wait_send()
+    down_load(0, 0).wait()
+    last = DIRECT - 1
+    s_last = (CHUNKS - 1) % SLOTS
+    gate_load(0, s_last).wait()
+    up_load(0, s_last).wait()
+    for j in range(1, NODES):
+        rows_copy(out1, in1, d_s, d_r, last, j).wait_recv()
+
+    @pl.loop(0, 4)
+    def _(t):
+        tile = block(t, BAND)
+        rows = in1[last, tile]
+        gate = acc_g[tile] + dot(rows, wgu[s_last, 0])
+        up = acc_u[tile] + dot(rows, wgu[s_last, 1])
+        hidden[tile] = silu_mul(gate, up).astype(BF16)
+        out1[0, tile] = dot(hidden[tile], wds[0]).astype(BF16)
+        for n in range(4):
+            j = (t + 4 - z) % 4 * 4 + (n + 4 - y) % 4
+
+            @pl.when(j != 0)
+            def _():
+                rows_copy(out1, in2, c_s, c_r, 0, j).start()
+
+    in2[0, mine] = out1[0, mine]
+    down_load(2, 0).start()
     for m in range(0, ROWS, ROW_TILE):
         hidden_a[m : m + ROW_TILE] = dot(square[m : m + ROW_TILE], hidden[...]).astype(BF16)
 
@@ -349,20 +378,15 @@
             xc_s.at[a, k], xc_r.at[a, k], (node, there),
         )
 
-    def next_down(c):
-        @pl.when(c + SLOTS < CHUNKS)
-        def _():
-            down_load(c + SLOTS, c % SLOTS).start()
-
     @pl.loop(0, ONCE)
     def _(a):
         for k in range(1, LOCALS):
             pass_copy(a, k).wait_send()
-        s = a % SLOTS
+        s = (a + 1) % SLOTS
         down_load(0, s).wait()
         for h in range(2):
             xo[a, h * ROWS : (h + 1) * ROWS] = dot(hidden_a[...], wds[s, :, h * WIDE : (h + 1) * WIDE]).astype(BF16)
-        next_down(a)
+        down_load(a + 4, s).start()
         for k in range(1, LOCALS):
             back_copy(a, k).start()
         xe[a, block(local, BAND)] = xo[a, block(core * 4 + x, BAND)]
@@ -377,22 +401,30 @@
             rows_copy(ao, ae, ac_s, ac_r, a, j).start()
         ae[a, mine] = ao[a, mine]
 
-    @pl.loop(0, DIRECT)
-    def _(b):
+    def direct_back(b):
         for j in range(1, NODES):
             rows_copy(out1, in1, d_s, d_r, b, j).wait_send()
-        c = b + ONCE
-        s = c % SLOTS
+        s = b % SLOTS
         down_load(0, s).wait()
         out1[b] = dot(hidden[...], wds[s]).astype(BF16)
-        next_down(c)
         for j in range(1, NODES):
             rows_copy(out1, in2, c_s, c_r, b, j).start()
         in2[b, mine] = out1[b, mine]
 
-        @pl.when(b >= 1)
-        def _():
-            node_sums(b - 1)
+    direct_back(1)
+
+    @pl.loop(0, ONCE)
+    def _(a):
+        hand_on(a)
+
+    @pl.loop(0, 2)
+    def _(a):
+        node_sums(a)
+        direct_back(a + 2)
+
+    @pl.loop(0, ONCE)
+    def _(a):
+        acc_s[...] += dot(gathered(a), ws[columns(a), :])
 
     hid_s[...] = silu_mul(acc_s[:, :SHARE], acc_s[:, SHARE:]).astype(BF16)
     loads[2].wait()
@@ -405,6 +437,9 @@
             held.at[c, core, tok_rows((x + k) % 4)], from_x.at[c, k], rx_s.at[c, k], rx_r.at[c, k], side(k)
         )
 
+    def extra_copy(a):
+        return remote(extra_out.at[a], extra.at[a, core], ex_s.at[a], ex_r.at[a], sib)
+
     def shared_part(c):
         for k in (1, 3, 2):
             gather_copy(c, k).wait_send()
@@ -419,41 +454,55 @@
         for k in (1, 3, 2):
             reduce_copy(c, k).start()
 
-    def finish(c):
+    def reduced(c):
         total = held[c, core, tok_rows(x)].astype(F32)
         for k in (1, 3, 2):
             reduce_copy(c, k).wait_recv()
             total = total + from_x[c, k].astype(F32)
-        out[:, columns(c)] = total.astype(BF16)
-
-    @pl.loop(0, DIRECT)
-    def _(i):
-        for j in range(1, NODES):
-            rows_copy(out1, in2, c_s, c_r, i, j).wait_recv()
-        c = i + ONCE
-        part = dot(mix[...], in2[i]) + shared_part(c)
+        return total
+
+    def finish(c):
+        out[:, columns(c)] = reduced(c).astype(BF16)
+
+    def finish_once(a):
+        total = reduced(a)
+        for j in range(1, NODES):
+            rows_copy(ao, ae, ac_s, ac_r, a, j).wait_recv()
+        sums = dot(mix_a[...], ae[a])
+        extra_out[a] = jnp.where(core == 0, sums[TOK:], sums[:TOK])
+        extra_copy(a).start()
+        extra[a, core] = jnp.where(core == 0, sums[:TOK], sums[TOK:])
+        extra_copy(a).wait_recv()
+        out[:, columns(a)] = (total + jnp.concatenate([extra[a, 0], extra[a, 1]], axis=1)).astype(BF16)
+
+    def direct_sums(b):
+        for j in range(1, NODES):
+            rows_copy(out1, in2, c_s, c_r, b, j).wait_recv()
+        c = b + ONCE
+        part = dot(mix[...], in2[b]) + shared_part(c)
         held[c] = part.astype(BF16).reshape(2, HALF, COLS)
         reduce(c)
 
-        @pl.when(i >= 2)
-        def _():
-            finish(i - 2)
-
-        @pl.when(i >= 1)
-        def _():
-            a = i - 1
-            for j in range(1, NODES):
-                rows_copy(ao, ae, ac_s, ac_r, a, j).wait_recv()
-            held[a] = shared_part(a).astype(BF16).reshape(2, HALF, COLS)
-            sums = dot(mix_a[...], ae[a])
-            for h in range(2):
-                old = held[a, h, tok_rows(x), wide].astype(F32)
-                held[a, h, tok_rows(x), wide] = (old + sums[h * TOK : (h + 1) * TOK]).astype(BF16)
-            reduce(a)
-
-        finish(c)
-
-    finish(ONCE - 1)
+    @pl.loop(0, ONCE)
+    def _(a):
+        held[a] = shared_part(a).astype(BF16).reshape(2, HALF, COLS)
+        reduce(a)
+
+    @pl.loop(0, 2)
+    def _(b):
+        direct_sums(b)
+
+    node_sums(2)
+    finish(ONCE)
+
+    @pl.loop(0, 2)
+    def _(i):
+        finish_once(i)
+        direct_sums(i + 2)
+        finish(ONCE + i + 1)
+
+    finish_once(2)
+    finish(CHUNKS - 1)
 
     @pl.loop(0, DIRECT)
     def _(b):
@@ -466,6 +515,7 @@
             back_copy(a, k).wait_send()
         for j in range(1, NODES):
             rows_copy(ao, ae, ac_s, ac_r, a, j).wait_send()
+        extra_copy(a).wait_send()
 
     @pl.loop(0, CHUNKS)
     def _(c):
@@ -518,6 +568,8 @@
             pltpu.VMEM((NODES, 2 * TOP, 128), F32),
             pltpu.VMEM((CHUNKS, HALF, COLS), BF16),
             pltpu.VMEM((CHUNKS, 4, TOK, COLS), BF16),
+            pltpu.VMEM((ONCE, TOK, WIDE), F32),
+            pltpu.VMEM((ONCE, 2, TOK, WIDE), F32),
             dma((3,)),
             dma((SLOTS, 2)),
             dma((SLOTS,)),
@@ -546,6 +598,8 @@
             dma((CHUNKS,)),
             dma((CHUNKS, 4)),
             dma((CHUNKS, 4)),
+            dma((ONCE,)),
+            dma((ONCE,)),
         ],
         compiler_params=pltpu.CompilerParams(
             collective_id=0, has_side_effects=True, vmem_limit_bytes=63 * 2**20

time: 151 us -> 136 us (0.901); the launches traced: 150 us -> 134 us
  Pallas kernels: 149 us -> 132 us
    pallas_call x1, Pallas kernels: 149 us -> 132 us  [on_device(): pl.pallas_call(kernel, out_shape=jax.ShapeDtypeStruct((TOK, D), BF16), in...]
where the time goes in v3:
time: 136 us; the launch traced here: 134 us
  Pallas kernels  132 us (97%)
  local copies, waits for them, and re-layouts  1.82 us (1%)
    pallas_call x1, Pallas kernels, on_device(): pl.pallas_call(kernel, out_shape=jax.ShapeDtypeStruct((TOK, D), BF16), in...  132 us

profile of v3, /device:TPU:9, one launch (start us, length us, event | category | flops | bytes accessed | tf_op | source)
XLA Modules:
  0.0 133.9 jit_solution(7121262349752079724)
XLA Ops:
  0.0 132.1 %moe.1 = bf16[64,3584]{1,0:T(8,128)(2,1)} custom-call(bf16[64,3584]{1,0:T(8,128)(2,1)} %tokens.1, s32[8,64]{1,0:T(8,128)} %bitcast.2, bf16[8,64]{1,0:T(8,128)(2,1)} %bitcast.3, bf16[1,3584,1024]{2,1,0:T(8,128)(2,1)} %eg.1, bf16[1,3584,1024]{2,1,0:T(8,128)(2,1)} %eu.1, bf16[1,1024,3584]{2,1,0:T(8,128)(2,1)} %ed.1, bf16[3584,128]{1,0:T(8,128)(2,1)} %sg.1, ...), custom_call_target="tpu_custom_call" | custom-call | flops 32000000000 | bytes 26000000 | tf_op jit(solution)/shard_map/moe/pallas_call | solution.py:531
  132.1 1.8 %copy.11 = bf16[64,3584]{1,0:T(8,128)(2,1)} copy(bf16[64,3584]{1,0:T(8,128)(2,1)} %moe.1) | data formatting | bytes 917504

commit v4 on v3

v4 whole, which is shorter than its diff:
```python
import jax
import jax.numpy as jnp
from jax import lax
from jax.experimental import pallas as pl
from jax.experimental.pallas import tpu as pltpu
from jax.sharding import PartitionSpec as P

MESH = pl.DeviceIdType.MESH
BF16 = jnp.bfloat16
F32 = jnp.float32

D = 3584
H = 1024
TOP = 8
TOK = 64
NODES = 16
LOCALS = 8
GROUP = TOK * LOCALS
PAIR = 2 * TOK
SLOT = 48
PART = 12
BAND = NODES * PART
ROWS = NODES * SLOT
SPREAD = LOCALS * BAND
COLS = 512
WIDE = COLS // 2
CHUNKS = D // COLS
ONCE = 3
DIRECT = CHUNKS - ONCE
HALF = GROUP // 2
SHARE = 128
ROW_TILE = 256
SLOTS = 3


def dot(a, b):
    return jnp.dot(a, b, preferred_element_type=F32)


def silu_mul(gate, up):
    return gate / (1.0 + jnp.exp(-gate)) * up


def count(shape, dim):
    return lax.broadcasted_iota(jnp.int32, shape, dim).astype(F32)


def quotient(values, by):
    return jnp.floor((values + 0.5) * (1.0 / by))


def ones_where(condition):
    return jnp.where(condition, 1.0, 0.0)


def kernel(
    tokens, ids, weights, eg, eu, ed, sg, su, sd, out,
    held, out1, in1, in2, ao, ai, ae, xo, xi, xe, acc_g, acc_u, hidden, hidden_a, wgu, wds, ws, wsd, acc_s, hid_s,
    pick, mix, pick_a, mix_a, spread, merge, square, work, meta, meta_all, slots_out, slots_in, from_sib, from_x, extra_out, extra, out_v,
    load_sem, gu_sem, wd_sem, own_sem, meta_s, meta_r, sm_s, sm_r, ag_s, ag_r, fw_s, fw_r, own_s, own_r,
    d_s, d_r, c_s, c_r, ad_s, ad_r, ac_s, ac_r, xd_s, xd_r, xc_s, xc_r, rs_s, rs_r, rx_s, rx_r, ex_s, ex_r, out_sem,
):
    node = lax.axis_index("node")
    local = lax.axis_index("local")
    z, y, x, core = node // 4, node % 4, local // 2, local % 2
    sib = (node, 2 * x + (1 - core))

    def far(j):
        return ((z + j // 4) % 4) * 4 + (y + j % 4) % 4

    def side(k):
        return (node, 2 * ((x + k) % 4) + core)

    def mate(k):
        return (local + k) % LOCALS

    def block(i, size):
        return pl.ds(pl.multiple_of(i * size, size), size)

    def by_tiles(rows, work_on):
        @pl.loop(0, rows // ROW_TILE)
        def _(i):
            work_on(block(i, ROW_TILE))

    def columns(c):
        return block(c, COLS)

    def tok_rows(i):
        return block(i, TOK)

    def remote(src, dst, send, recv, device):
        return pltpu.make_async_remote_copy(
            src_ref=src, dst_ref=dst, send_sem=send, recv_sem=recv, device_id=device, device_id_type=MESH
        )

    def settled(ref, sem):
        pltpu.make_async_copy(ref, ref, sem).wait()

    barrier = pltpu.get_barrier_semaphore()
    for j in range(1, NODES):
        pl.semaphore_signal(barrier, inc=1, device_id=(far(j), local), device_id_type=MESH)
    for k in range(1, LOCALS):
        pl.semaphore_signal(barrier, inc=1, device_id=(node, mate(k)), device_id_type=MESH)

    loads = [
        pltpu.make_async_copy(sg, ws.at[:, pl.ds(0, SHARE)], load_sem.at[0]),
        pltpu.make_async_copy(su, ws.at[:, pl.ds(SHARE, SHARE)], load_sem.at[1]),
        pltpu.make_async_copy(sd, wsd, load_sem.at[2]),
    ]

    def own_copy(c):
        return pltpu.make_async_copy(tokens.at[:, columns(c)], held.at[c, core, tok_rows(x)], own_sem.at[c])

    def gate_load(c, s):
        return pltpu.make_async_copy(eg.at[0, columns(c)], wgu.at[s, 0], gu_sem.at[s, 0])

    def up_load(c, s):
        return pltpu.make_async_copy(eu.at[0, columns(c)], wgu.at[s, 1], gu_sem.at[s, 1])

    def down_load(c, s):
        return pltpu.make_async_copy(ed.at[0, :, columns(c)], wds.at[s], wd_sem.at[s])

    def in_turn(q):
        return (1 - q % 2) * ONCE + q // 2

    for c in range(CHUNKS):
        own_copy(c).start()

    meta[...] = jnp.zeros_like(meta)
    meta[0:TOP, 0:TOK] = ids[...].astype(F32) + 1.0
    meta[TOP : 2 * TOP, 0:TOK] = weights[...].astype(F32)

    pl.semaphore_wait(barrier, NODES - 1 + LOCALS - 1)

    def meta_copy(k, s):
        return remote(meta, meta_all.at[core * 4 + x], meta_s.at[s], meta_r.at[s], (node, mate(k)))

    def gather_copy(c, k):
        return remote(tokens.at[:, columns(c)], held.at[c, core, tok_rows(x)], ag_s.at[c], ag_r.at[c], side(k))

    def forward_copy(c, k):
        mid = held.at[c, core, tok_rows((x + 4 - k) % 4)]
        if k == 0:
            return remote(tokens.at[:, columns(c)], mid, own_s.at[c], own_r.at[c], sib)
        return remote(mid, mid, fw_s.at[c], fw_r.at[c], sib)

    def three_wait(sem, c):
        settled(held.at[c, 0, pl.ds(0, 3 * TOK)], sem.at[c])

    to_sib = 1 + 6 * core
    meta_copy(to_sib, 0).start()
    for c in range(CHUNKS):
        forward_copy(c, 0).start()
    for k in range(2, LOCALS - 1):
        meta_copy(k, 1).start()
    meta_copy(LOCALS - to_sib, 1).start()

    @pl.loop(0, CHUNKS)
    def _(i):
        for k in (1, 3, 2):
            gather_copy((i + ONCE) % CHUNKS, k).start()

    meta_all[core * 4 + x] = meta[...]
    meta_copy(to_sib, 0).wait_recv()

    chip_table = jnp.concatenate([meta_all[x][:, :TOK], meta_all[4 + x][:, :TOK]], axis=1)
    chip_node = quotient(chip_table[:TOP] - 1.0, LOCALS)
    node_row = count((NODES, PAIR), 0)
    chosen = jnp.zeros((NODES, PAIR), F32)
    for k in range(0, TOP, 2):
        chosen = chosen + ones_where(chip_node[k : k + 1] == node_row)
    earlier = count((PAIR, PAIR), 0) < count((PAIR, PAIR), 1)
    rank_a = dot(chosen.astype(BF16), ones_where(earlier).astype(BF16))
    rank_a = jnp.where(chosen > 0.5, rank_a, -1.0)
    place_a = count((SLOT, PAIR), 0)
    for n in range(NODES):
        pick_a[n * SLOT : (n + 1) * SLOT] = ones_where(rank_a[n : n + 1] == place_a).astype(BF16)

    def notes_copy(j):
        there = far(j)
        return remote(slots_out.at[there], slots_in.at[node], sm_s.at[0], sm_r.at[0], (there, local))

    def rows_copy(src, dst, send, recv, c, j):
        there = far(j)
        return remote(
            src.at[c, block(there, SLOT)], dst.at[c, block(node, SLOT)], send.at[c], recv.at[c], (there, local)
        )

    def rows_wait(ref, sem, c):
        settled(ref.at[c, pl.ds(0, (NODES - 1) * SLOT)], sem.at[c])

    def lanes_wait(ref, sem, a):
        settled(ref.at[a, pl.ds(0, (LOCALS - 1) * BAND)], sem.at[a])

    mine = block(node, SLOT)
    wide = block(core, WIDE)

    def once_rows(a):
        own_copy(a).wait()
        forward_copy(a, 0).wait_recv()
        rows = jnp.concatenate([held[a, 0, tok_rows(x), wide], held[a, 1, tok_rows(x), wide]], axis=0)
        ao[a] = dot(pick_a[...], rows).astype(BF16)
        for j in range(1, NODES):
            rows_copy(ao, ai, ad_s, ad_r, a, j).start()
        ai[a, mine] = ao[a, mine]

    once_rows(0)

    slots_out[...] = jnp.zeros_like(slots_out)
    notes = lax.dot_general(
        chip_table.astype(BF16), pick_a[...], (((1,), (1,)), ((), ())), preferred_element_type=F32
    )
    for n in range(NODES):
        slots_out[n, :, 0:SLOT] = notes[:, n * SLOT : (n + 1) * SLOT]

    for j in range(1, NODES):
        notes_copy(j).start()
    slots_in[node] = slots_out[node]

    @pl.loop(1, ONCE)
    def _(a):
        once_rows(a)

    for load in loads:
        load.start()
    for s in range(SLOTS):
        gate_load(in_turn(s), s).start()
        up_load(in_turn(s), s).start()
    for s, c in enumerate((ONCE, 0, 1)):
        down_load(c, s).start()

    def hand_on(c):
        three_wait(ag_r, c)
        for k in (1, 3, 2):
            forward_copy(c, k).start()

    def gathered(c):
        three_wait(fw_r, c)

    def shared_add(c):
        @pl.loop(0, 2)
        def _(h):
            acc_s[block(h, HALF)] += dot(held[c, h], ws[columns(c), :])

    def direct_rows(b):
        c = b + ONCE
        own_copy(c).wait()
        forward_copy(c, 0).wait_recv()
        hand_on(c)
        gathered(c)

        def select(tile):
            out1[b, tile] = dot(pick[tile], held[c].reshape(GROUP, COLS)).astype(BF16)

        by_tiles(ROWS, select)
        for j in range(1, NODES):
            rows_copy(out1, in1, d_s, d_r, b, j).start()
        in1[b, mine] = out1[b, mine]
        shared_add(c)

    def pass_copy(a, k):
        there = mate(k)
        return remote(
            xo.at[a, block(there, BAND)], xi.at[a, block(core * 4 + x, BAND)], xd_s.at[a], xd_r.at[a], (node, there)
        )

    def pass_rows(a):
        rows_wait(ai, ad_r, a)

        def select(tile):
            xo[a, tile] = dot(spread[tile], ai[a]).astype(BF16)

        by_tiles(SPREAD, select)
        for k in range(1, LOCALS):
            pass_copy(a, k).start()
        xi[a, block(core * 4 + x, BAND)] = xo[a, block(local, BAND)]

    first, then = count((ROWS, 1), 0), count((1, ROWS), 1)
    earlier = (first < then) & (quotient(first, SLOT) == quotient(then, SLOT))
    square[...] = ones_where(earlier).astype(BF16)

    settled(slots_in.at[pl.ds(0, NODES - 1)], sm_s.at[0])
    settled(slots_in.at[pl.ds(0, NODES - 1)], sm_r.at[0])
    slot_table = jnp.concatenate([slots_in[n][:, :SLOT] for n in range(NODES)], axis=1)
    expert = count((LOCALS, ROWS), 0) + (node * LOCALS + 1).astype(F32)
    chosen = jnp.zeros((LOCALS, ROWS), F32)
    gain_a = jnp.zeros((LOCALS, ROWS), F32)
    for k in range(TOP):
        hit = ones_where(slot_table[k : k + 1] == expert)
        chosen = chosen + hit
        gain_a = gain_a + hit * slot_table[TOP + k : TOP + k + 1]
    slot_row = count((1, ROWS), 1)
    seat = dot(chosen.astype(BF16), square[...]) + quotient(slot_row, SLOT) * PART
    seat = jnp.where(chosen > 0.5, seat, -1.0)
    place_x = count((BAND, ROWS), 0)
    for l in range(LOCALS):
        spread[l * BAND : (l + 1) * BAND] = ones_where(seat[l : l + 1] == place_x).astype(BF16)

    meta_copy(to_sib, 0).wait_send()
    settled(meta_all.at[pl.ds(0, LOCALS - 2)], meta_s.at[1])
    settled(meta_all.at[pl.ds(0, LOCALS - 2)], meta_r.at[1])

    table = jnp.concatenate([meta_all[d][:, :TOK] for d in range(LOCALS)], axis=1)
    expert = count((NODES, GROUP), 0) * LOCALS + (local + 1).astype(F32)
    chosen = jnp.zeros((NODES, GROUP), F32)
    gain = jnp.zeros((NODES, GROUP), F32)
    for k in range(TOP):
        hit = ones_where(table[k : k + 1] == expert)
        chosen = chosen + hit
        gain = gain + hit * table[TOP + k : TOP + k + 1]

    def chip_of(t):
        device = quotient(t, TOK)
        return device - 4.0 * quotient(device, 4)

    first, then = count((GROUP, 1), 0), count((1, GROUP), 1)
    earlier = (first < then) & (chip_of(first) == chip_of(then))
    rank = dot(chosen.astype(BF16), ones_where(earlier).astype(BF16)) + chip_of(then) * PART
    rank = jnp.where(chosen > 0.5, rank, -1.0)
    place = count((SLOT, GROUP), 0)
    for n in range(NODES):
        pick[n * SLOT : (n + 1) * SLOT] = ones_where(rank[n : n + 1] == place).astype(BF16)

    acc_s[...] = jnp.zeros_like(acc_s)
    loads[0].wait()
    loads[1].wait()

    @pl.loop(0, DIRECT)
    def _(b):
        @pl.when(b < ONCE)
        def _():
            pass_rows(b)

        direct_rows(b)

    @pl.loop(0, ONCE)
    def _(a):
        hand_on(a)

    @pl.loop(0, ONCE)
    def _(a):
        gathered(a)
        shared_add(a)

    hid_s[...] = silu_mul(acc_s[:, :SHARE], acc_s[:, SHARE:]).astype(BF16)
    loads[2].wait()

    def sib_copy(c):
        return remote(held.at[c, 1 - core], from_sib.at[c], rs_s.at[c], rs_r.at[c], sib)

    def reduce_copy(c, k):
        return remote(
            held.at[c, core, tok_rows((x + k) % 4)], from_x.at[c, k], rx_s.at[c], rx_r.at[c], side(k)
        )

    def extra_copy(a):
        return remote(extra_out.at[a], extra.at[a, core], ex_s.at[a], ex_r.at[a], sib)

    def gather_sent(c):
        three_wait(ag_s, c)
        three_wait(fw_s, c)
        forward_copy(c, 0).wait_send()

    def shared_part(c, h):
        return dot(hid_s[block(h, HALF)], wsd[:, columns(c)])

    def reduce(c):
        sib_copy(c).start()
        sib_copy(c).wait_recv()
        held[c, core] = (held[c, core].astype(F32) + from_sib[c].astype(F32)).astype(BF16)
        for k in (1, 3, 2):
            reduce_copy(c, k).start()

    def reduced(c):
        total = held[c, core, tok_rows(x)].astype(F32)
        settled(from_x.at[c, pl.ds(1, 3)], rx_r.at[c])
        for k in (1, 3, 2):
            total = total + from_x[c, k].astype(F32)
        return total

    def out_copy(c):
        return pltpu.make_async_copy(out_v.at[c], out.at[:, columns(c)], out_sem.at[c])

    def finish(c):
        out_v[c] = reduced(c).astype(BF16)
        out_copy(c).start()

    def finish_once(a):
        total = reduced(a)
        rows_wait(ae, ac_r, a)
        sums = dot(mix_a[...], ae[a])
        extra_out[a] = jnp.where(core == 0, sums[TOK:], sums[:TOK])
        extra_copy(a).start()
        extra[a, core] = jnp.where(core == 0, sums[:TOK], sums[TOK:])
        extra_copy(a).wait_recv()
        out_v[a] = (total + jnp.concatenate([extra[a, 0], extra[a, 1]], axis=1)).astype(BF16)
        out_copy(a).start()

    def direct_sums(b):
        rows_wait(in2, c_r, b)
        c = b + ONCE
        gather_sent(c)

        @pl.loop(0, 2)
        def _(h):
            held[c, h] = (dot(mix[block(h, HALF)], in2[b]) + shared_part(c, h)).astype(BF16)

        reduce(c)

    @pl.loop(0, ONCE)
    def _(a):
        gather_sent(a)

        @pl.loop(0, 2)
        def _(h):
            held[a, h] = shared_part(a, h).astype(BF16)

        reduce(a)

    def clear(tile):
        acc_g[tile] = jnp.zeros((ROW_TILE, H), F32)
        acc_u[tile] = jnp.zeros((ROW_TILE, H), F32)

    by_tiles(ROWS, clear)

    row, column = count((ROWS, 1), 0), count((1, ROWS), 1)
    by_node = quotient(row, SLOT)
    by_chip = quotient(row - by_node * SLOT, PART)
    square[...] = ones_where(row - by_node * SLOT - by_chip * PART + by_chip * BAND + by_node * PART == column).astype(BF16)
    for n in range(NODES):
        hit = jnp.where(rank[n : n + 1] == place, gain[n : n + 1], 0.0)
        mix[:, n * SLOT : (n + 1) * SLOT] = jnp.transpose(hit).astype(BF16)
    for n in range(0, NODES, 8):
        hits = [ones_where(rank_a[i : i + 1] == place_a) for i in range(n, n + 8)]
        mix_a[:, n * SLOT : (n + 8) * SLOT] = jnp.transpose(jnp.concatenate(hits, axis=0)).astype(BF16)
    for l in range(0, LOCALS, 2):
        hits = [jnp.where(seat[i : i + 1] == place_x, gain_a[i : i + 1], 0.0) for i in (l, l + 1)]
        merge[:, l * BAND : (l + 2) * BAND] = jnp.transpose(jnp.concatenate(hits, axis=0)).astype(BF16)

    def gate_up(q, get):
        s = q % SLOTS
        gate_load(0, s).wait()
        up_load(0, s).wait()

        def add(tile):
            rows = get(tile)
            acc_g[tile] += dot(rows, wgu[s, 0])
            acc_u[tile] += dot(rows, wgu[s, 1])

        by_tiles(ROWS, add)

        @pl.when(q + SLOTS < CHUNKS)
        def _():
            gate_load(in_turn(q + SLOTS), s).start()
            up_load(in_turn(q + SLOTS), s).start()

    @pl.loop(0, ONCE)
    def _(i):
        rows_wait(in1, d_r, i)
        gate_up(2 * i, lambda tile: in1[i, tile])
        lanes_wait(xi, xd_r, i)

        def reorder(tile):
            for h in range(2):
                work[tile, h * WIDE : (h + 1) * WIDE] = dot(square[tile], xi[i, h * ROWS : (h + 1) * ROWS]).astype(BF16)

        by_tiles(ROWS, reorder)
        gate_up(2 * i + 1, lambda tile: work[tile])

    by_chip = quotient(row, BAND)
    by_node = quotient(row - by_chip * BAND, PART)
    square[...] = ones_where(row - by_chip * BAND - by_node * PART + by_node * SLOT + by_chip * PART == column).astype(BF16)

    rows_wait(out1, d_s, 0)
    down_load(0, 0).wait()
    last = DIRECT - 1
    s_last = (CHUNKS - 1) % SLOTS
    gate_load(0, s_last).wait()
    up_load(0, s_last).wait()
    rows_wait(in1, d_r, last)

    @pl.loop(0, 4)
    def _(t):
        tile = block(t, BAND)
        rows = in1[last, tile]
        gate = acc_g[tile] + dot(rows, wgu[s_last, 0])
        up = acc_u[tile] + dot(rows, wgu[s_last, 1])
        hidden[tile] = silu_mul(gate, up).astype(BF16)
        out1[0, tile] = dot(hidden[tile], wds[0]).astype(BF16)
        for n in range(4):
            j = (t + 4 - z) % 4 * 4 + (n + 4 - y) % 4

            @pl.when(j != 0)
            def _():
                rows_copy(out1, in2, c_s, c_r, 0, j).start()

    in2[0, mine] = out1[0, mine]
    down_load(2, 0).start()

    def reorder_hidden(tile):
        hidden_a[tile] = dot(square[tile], hidden[...]).astype(BF16)

    by_tiles(ROWS, reorder_hidden)

    def back_copy(a, k):
        there = mate(k)
        return remote(
            xo.at[a, block(there % 2 * 4 + there // 2, BAND)], xe.at[a, block(local, BAND)],
            xc_s.at[a], xc_r.at[a], (node, there),
        )

    @pl.loop(0, ONCE)
    def _(a):
        lanes_wait(xo, xd_s, a)
        s = (a + 1) % SLOTS
        down_load(0, s).wait()

        @pl.loop(0, ROWS // ROW_TILE)
        def _(i):
            for h in range(2):
                part = dot(hidden_a[block(i, ROW_TILE)], wds[s, :, h * WIDE : (h + 1) * WIDE])
                xo[a, block(h * (ROWS // ROW_TILE) + i, ROW_TILE)] = part.astype(BF16)

        down_load(a + 4, s).start()
        for k in range(1, LOCALS):
            back_copy(a, k).start()
        xe[a, block(local, BAND)] = xo[a, block(core * 4 + x, BAND)]

    def node_sums(a):
        rows_wait(ao, ad_s, a)
        lanes_wait(xe, xc_r, a)

        def add(tile):
            ao[a, tile] = dot(merge[tile], xe[a]).astype(BF16)

        by_tiles(ROWS, add)
        for j in range(1, NODES):
            rows_copy(ao, ae, ac_s, ac_r, a, j).start()
        ae[a, mine] = ao[a, mine]

    def direct_back(b):
        rows_wait(out1, d_s, b)
        s = b % SLOTS
        down_load(0, s).wait()

        def down(tile):
            out1[b, tile] = dot(hidden[tile], wds[s]).astype(BF16)

        by_tiles(ROWS, down)
        for j in range(1, NODES):
            rows_copy(out1, in2, c_s, c_r, b, j).start()
        in2[b, mine] = out1[b, mine]

    @pl.loop(1, DIRECT)
    def _(b):
        @pl.when(b > 1)
        def _():
            node_sums(b - 2)

        direct_back(b)

    @pl.loop(0, DIRECT)
    def _(b):
        @pl.when(b == 2)
        def _():
            node_sums(ONCE - 1)

        @pl.when(b >= 2)
        def _():
            finish_once(b - 2)

        direct_sums(b)

        @pl.when(b >= 1)
        def _():
            finish(ONCE + b - 1)

    finish_once(ONCE - 1)
    finish(CHUNKS - 1)

    @pl.loop(0, DIRECT)
    def _(b):
        rows_wait(out1, c_s, b)

    @pl.loop(0, ONCE)
    def _(a):
        lanes_wait(xo, xc_s, a)
        rows_wait(ao, ac_s, a)
        extra_copy(a).wait_send()

    @pl.loop(0, CHUNKS)
    def _(c):
        sib_copy(c).wait_send()
        settled(from_x.at[c, pl.ds(1, 3)], rx_s.at[c])
        out_copy(c).wait()


def on_device(tokens, ids, weights, *matrices):
    vmem = pl.BlockSpec(memory_space=pltpu.VMEM)
    hbm = pl.BlockSpec(memory_space=pl.ANY)
    dma = pltpu.SemaphoreType.DMA
    return pl.pallas_call(
        kernel,
        out_shape=jax.ShapeDtypeStruct((TOK, D), BF16),
        in_specs=[hbm, vmem, vmem] + [hbm] * 6,
        out_specs=hbm,
        scratch_shapes=[
            pltpu.VMEM((CHUNKS, 2, HALF, COLS), BF16),
            pltpu.VMEM((DIRECT, ROWS, COLS), BF16),
            pltpu.VMEM((DIRECT, ROWS, COLS), BF16),
            pltpu.VMEM((DIRECT, ROWS, COLS), BF16),
            pltpu.VMEM((ONCE, ROWS, WIDE), BF16),
            pltpu.VMEM((ONCE, ROWS, WIDE), BF16),
            pltpu.VMEM((ONCE, ROWS, WIDE), BF16),
            pltpu.VMEM((ONCE, SPREAD, WIDE), BF16),
            pltpu.VMEM((ONCE, SPREAD, WIDE), BF16),
            pltpu.VMEM((ONCE, SPREAD, WIDE), BF16),
            pltpu.VMEM((ROWS, H), F32),
            pltpu.VMEM((ROWS, H), F32),
            pltpu.VMEM((ROWS, H), BF16),
            pltpu.VMEM((ROWS, H), BF16),
            pltpu.VMEM((SLOTS, 2, COLS, H), BF16),
            pltpu.VMEM((SLOTS, H, COLS), BF16),
            pltpu.VMEM((D, 2 * SHARE), BF16),
            pltpu.VMEM((SHARE, D), BF16),
            pltpu.VMEM((GROUP, 2 * SHARE), F32),
            pltpu.VMEM((GROUP, SHARE), BF16),
            pltpu.VMEM((ROWS, GROUP), BF16),
            pltpu.VMEM((GROUP, ROWS), BF16),
            pltpu.VMEM((ROWS, PAIR), BF16),
            pltpu.VMEM((PAIR, ROWS), BF16),
            pltpu.VMEM((SPREAD, ROWS), BF16),
            pltpu.VMEM((ROWS, SPREAD), BF16),
            pltpu.VMEM((ROWS, ROWS), BF16),
            pltpu.VMEM((ROWS, COLS), BF16),
            pltpu.VMEM((2 * TOP, 128), F32),
            pltpu.VMEM((LOCALS, 2 * TOP, 128), F32),
            pltpu.VMEM((NODES, 2 * TOP, 128), F32),
            pltpu.VMEM((NODES, 2 * TOP, 128), F32),
            pltpu.VMEM((CHUNKS, HALF, COLS), BF16),
            pltpu.VMEM((CHUNKS, 4, TOK, COLS), BF16),
            pltpu.VMEM((ONCE, TOK, WIDE), F32),
            pltpu.VMEM((ONCE, 2, TOK, WIDE), F32),
            pltpu.VMEM((CHUNKS, TOK, COLS), BF16),
            dma((3,)),
            dma((SLOTS, 2)),
            dma((SLOTS,)),
            dma((CHUNKS,)),
            dma((2,)),
            dma((2,)),
            dma((1,)),
            dma((1,)),
            dma((CHUNKS,)),
            dma((CHUNKS,)),
            dma((CHUNKS,)),
            dma((CHUNKS,)),
            dma((CHUNKS,)),
            dma((CHUNKS,)),
            dma((DIRECT,)),
            dma((DIRECT,)),
            dma((DIRECT,)),
            dma((DIRECT,)),
            dma((ONCE,)),
            dma((ONCE,)),
            dma((ONCE,)),
            dma((ONCE,)),
            dma((ONCE,)),
            dma((ONCE,)),
            dma((ONCE,)),
            dma((ONCE,)),
            dma((CHUNKS,)),
            dma((CHUNKS,)),
            dma((CHUNKS,)),
            dma((CHUNKS,)),
            dma((ONCE,)),
            dma((ONCE,)),
            dma((CHUNKS,)),
        ],
        compiler_params=pltpu.CompilerParams(
            collective_id=0, has_side_effects=True, vmem_limit_bytes=63 * 2**20
        ),
        cost_estimate=pl.CostEstimate(flops=32 * 10**9, bytes_accessed=26 * 10**6, transcendentals=10**6),
        name="moe",
    )(tokens, ids.T, weights.T, *matrices)


def solution(mesh):
    both = ("node", "local")
    in_specs = (
        P(both, None),
        P(both, None),
        P(both, None),
        P(both, None, None),
        P(both, None, None),
        P(both, None, None),
        P(None, "local"),
        P(None, "local"),
        P("local", None),
    )
    return jax.shard_map(on_device, mesh=mesh, in_specs=in_specs, out_specs=P(both, None), check_vma=False)
```

time: 136 us -> 127 us (0.934)
  Pallas kernels: 132 us -> 124 us
    pallas_call x1, Pallas kernels: 132 us -> 124 us  [on_device(): pl.pallas_call(kernel, out_shape=jax.ShapeDtypeStruct((TOK, D), BF16), in...]
where the time goes in v4:
time: 127 us; the launch traced here: 126 us
  Pallas kernels  124 us (98%)
  local copies, waits for them, and re-layouts  1.82 us (1%)
    pallas_call x1, Pallas kernels, on_device(): pl.pallas_call(kernel, out_shape=jax.ShapeDtypeStruct((TOK, D), BF16), in...  124 us

profile of v4, /device:TPU:9, one launch (start us, length us, event | category | flops | bytes accessed | tf_op | source)
XLA Modules:
  0.0 125.8 jit_solution(4578662502567702968)
XLA Ops:
  0.0 124.0 %moe.1 = bf16[64,3584]{1,0:T(8,128)(2,1)} custom-call(bf16[64,3584]{1,0:T(8,128)(2,1)} %tokens.1, s32[8,64]{1,0:T(8,128)} %bitcast.2, bf16[8,64]{1,0:T(8,128)(2,1)} %bitcast.3, bf16[1,3584,1024]{2,1,0:T(8,128)(2,1)} %eg.1, bf16[1,3584,1024]{2,1,0:T(8,128)(2,1)} %eu.1, bf16[1,1024,3584]{2,1,0:T(8,128)(2,1)} %ed.1, bf16[3584,128]{1,0:T(8,128)(2,1)} %sg.1, ...), custom_call_target="tpu_custom_call" | custom-call | flops 32000000000 | bytes 26000000 | tf_op jit(solution)/shard_map/moe/pallas_call | solution.py:602
  124.0 1.8 %copy.11 = bf16[64,3584]{1,0:T(8,128)(2,1)} copy(bf16[64,3584]{1,0:T(8,128)(2,1)} %moe.1) | data formatting | bytes 917504

commit v5 on v4

--- a/solution.py
+++ b/solution.py
@@ -29,7 +29,7 @@
 DIRECT = CHUNKS - ONCE
 HALF = GROUP // 2
 SHARE = 128
-ROW_TILE = 256
+ROW_TILE = 384
 SLOTS = 3
 
 

time: 127 us -> 128 us (level)
  no operation moved by 1% of the time
where the time goes in v5:
time: 128 us; the launch traced here: 126 us
  Pallas kernels  124 us (97%)
  local copies, waits for them, and re-layouts  1.82 us (1%)
    pallas_call x1, Pallas kernels, on_device(): pl.pallas_call(kernel, out_shape=jax.ShapeDtypeStruct((TOK, D), BF16), in...  124 us

profile of v5, /device:TPU:9, one launch (start us, length us, event | category | flops | bytes accessed | tf_op | source)
XLA Modules:
  0.0 125.7 jit_solution(2651682923604942944)
XLA Ops:
  0.0 123.9 %moe.1 = bf16[64,3584]{1,0:T(8,128)(2,1)} custom-call(bf16[64,3584]{1,0:T(8,128)(2,1)} %tokens.1, s32[8,64]{1,0:T(8,128)} %bitcast.2, bf16[8,64]{1,0:T(8,128)(2,1)} %bitcast.3, bf16[1,3584,1024]{2,1,0:T(8,128)(2,1)} %eg.1, bf16[1,3584,1024]{2,1,0:T(8,128)(2,1)} %eu.1, bf16[1,1024,3584]{2,1,0:T(8,128)(2,1)} %ed.1, bf16[3584,128]{1,0:T(8,128)(2,1)} %sg.1, ...), custom_call_target="tpu_custom_call" | custom-call | flops 32000000000 | bytes 26000000 | tf_op jit(solution)/shard_map/moe/pallas_call | solution.py:602
  123.9 1.8 %copy.11 = bf16[64,3584]{1,0:T(8,128)(2,1)} copy(bf16[64,3584]{1,0:T(8,128)(2,1)} %moe.1) | data formatting | bytes 917504
